TPU v7x, 32 devices: a whole 2x2x4 slice. The times are simulated.
32 devices in a mesh: node: 8 (over y, x, core), group: 4 (over z).
Axes of the slice: x: 2, y: 2, z: 4, core: 2. Of those that a mesh axis runs over, the one named last changes fastest.
Arguments:
- tokens: bfloat16 [8192, 1024], P(('node', 'group')), may hold values from -6 to 6
- grad_out: bfloat16 [8192, 1024], P(('node', 'group')), may hold values from -1.5 to 1.5
- router_gate: float32 [8192, 1], P(('node', 'group')), may hold values from 0.1 to 1
- counts: int32 [32], P(('node', 'group')), may hold values from 1 to 2
- routes: int32 [32, 2, 1], P(('node', 'group')), may hold values from 0 to 3, as said below
- partner: int32 [8], replicated, may hold values from 0 to 7, as said below
- w_gate: bfloat16 [32, 1024, 256], P(('node', 'group')), may hold values from -0.1875 to 0.1875
- w_up: bfloat16 [32, 1024, 256], P(('node', 'group')), may hold values from -0.1875 to 0.1875
- w_down: bfloat16 [32, 256, 1024], P(('node', 'group')), may hold values from -0.375 to 0.375
Outputs:
- grad_tokens: bfloat16 [8192, 1024], P(('node', 'group'))
- grad_gate: bfloat16 [32, 1024, 256], P(('node', 'group'))
- grad_up: bfloat16 [32, 1024, 256], P(('node', 'group'))
- grad_down: bfloat16 [32, 256, 1024], P(('node', 'group'))
Inputs may be any that keep to these rules, and one draw needn't show every extreme that they name: `routes`: the 2 entries of one device name different devices of its group; every device of a group is named; in every node group one device is named by exactly 3 entries and none by more. partner pairs the nodes: partner[partner[n]] = n and partner[n] != n.
All inputs are finite; a program needn't handle non-finite values.
Results may differ from a plain program's by a relative error of at most 0.015.
Values may be sent and summed in bfloat16 or wider, within the bound.
No kernel may reach another device: no remote copies, remote signals or barrier semaphores. Data moves between devices by JAX's collectives and lax.ppermute only.
A program may use at most 128 MiB of HBM per device.

v0:
```python
import jax
import jax.numpy as jnp
from jax import lax
from jax.sharding import PartitionSpec as P


def against(left, right):
    return lax.dot_general(
        left, right, (((1,), (1,)), ((), ())), preferred_element_type=jnp.float32
    )


def across(left, right):
    return lax.dot_general(
        left, right, (((0,), (0,)), ((), ())), preferred_element_type=jnp.float32
    )


def forward_pass(rows, w_gate, w_up):
    gate_pre = jnp.dot(rows, w_gate, preferred_element_type=jnp.float32)
    up_pre = jnp.dot(rows, w_up, preferred_element_type=jnp.float32)
    sigmoid = jax.nn.sigmoid(gate_pre)
    swish = gate_pre * sigmoid
    hidden = (swish * up_pre).astype(jnp.bfloat16)
    return (gate_pre, up_pre, sigmoid, swish, hidden)


def relocate(w_gate, w_up, w_down, partner):
    nodes = lax.axis_size("node")
    depth, width = (w_gate.shape[1], w_gate.shape[2])
    gate_parts = w_gate.reshape(nodes, depth // nodes, width)
    up_parts = w_up.reshape(nodes, depth // nodes, width)
    down_parts = w_down.reshape(nodes, width // nodes, depth)
    mixed = (
        lax.all_to_all(gate_parts, "node", split_axis=0, concat_axis=0, tiled=True),
        lax.all_to_all(up_parts, "node", split_axis=0, concat_axis=0, tiled=True),
        lax.all_to_all(down_parts, "node", split_axis=0, concat_axis=0, tiled=True),
    )
    gate_pick = jnp.take(mixed[0], partner, axis=0)
    up_pick = jnp.take(mixed[1], partner, axis=0)
    down_pick = jnp.take(mixed[2], partner, axis=0)
    placed = (
        lax.all_to_all(gate_pick, "node", split_axis=0, concat_axis=0, tiled=True),
        lax.all_to_all(up_pick, "node", split_axis=0, concat_axis=0, tiled=True),
        lax.all_to_all(down_pick, "node", split_axis=0, concat_axis=0, tiled=True),
    )
    return (
        placed[0].reshape(depth, width),
        placed[1].reshape(depth, width),
        placed[2].reshape(width, depth),
    )


def on_device(tokens, grad_out, router_gate, counts, routes, partner, w_gate, w_up, w_down):
    group = lax.axis_size("group")
    slots_dev, topk = (routes.shape[1], routes.shape[2])
    spread = slots_dev * topk
    capacity = spread + spread // 2
    block = tokens.shape[0] // slots_dev
    depth = tokens.shape[1]
    shard_rows = slots_dev * block
    placed_gate, placed_up, placed_down = relocate(w_gate, w_up, w_down, partner)
    live_rows = (jnp.arange(shard_rows, dtype=jnp.int32) // block < counts[0])[:, None]
    masked_tok = jnp.where(live_rows, tokens, jnp.zeros((), jnp.bfloat16))
    masked_out = jnp.where(live_rows, grad_out, jnp.zeros((), jnp.bfloat16))
    table = lax.all_gather(routes, "group", axis=0, tiled=True)
    myself = lax.axis_index("group")
    flat = table.reshape(group * spread)
    chosen = flat == myself
    index = jnp.argsort(jnp.where(chosen, 0, 1).astype(jnp.int32), stable=True)[:capacity]
    valid = chosen[index]
    sources = index // spread
    own_block = index % spread // topk
    column = index % topk
    targets = jnp.arange(group, dtype=jnp.int32)
    onehot = (routes[0][None, :, :] == targets[:, None, None]).astype(jnp.bfloat16)
    pick = ((sources[:, None] == targets[None, :]) & valid[:, None]).astype(jnp.bfloat16)
    wanted = sources * shard_rows + own_block * block
    column_hot = (jnp.arange(topk, dtype=jnp.int32)[None, :] == column[:, None]).astype(jnp.float32)
    empty = jnp.zeros((capacity, block, depth), jnp.bfloat16)
    tok_piece = lax.all_gather(masked_tok, "group", axis=0, tiled=True)
    out_piece = lax.all_gather(masked_out, "group", axis=0, tiled=True)
    gate_piece = lax.all_gather(
        router_gate.astype(jnp.bfloat16), "group", axis=0, tiled=True
    ).astype(jnp.float32)
    length = tok_piece.shape[0]
    inside = valid & (wanted >= 0) & (wanted + block <= length)
    offset = jnp.clip(wanted, 0, length - block)

    def take_one(where_at):
        return (
            lax.dynamic_slice_in_dim(tok_piece, where_at, block, 0),
            lax.dynamic_slice_in_dim(out_piece, where_at, block, 0),
            lax.dynamic_slice_in_dim(gate_piece, where_at, block, 0),
        )

    tok_sel, out_sel, gate_sel = jax.vmap(take_one)(offset)
    weight = jnp.sum(gate_sel * column_hot[:, None, :], axis=2)
    scaled_sel = (weight[:, :, None] * out_sel.astype(jnp.float32)).astype(jnp.bfloat16)
    keep = inside[:, None, None]
    got_tok = jnp.where(keep, tok_sel, empty)
    got_grad = jnp.where(keep, scaled_sel, empty)
    rows = got_tok.reshape(capacity * block, depth)
    grads = got_grad.reshape(capacity * block, depth)
    gate_pre, up_pre, sigmoid, swish, hidden = forward_pass(rows, placed_gate, placed_up)
    grad_hidden = against(grads, placed_down)
    grad_upre = (grad_hidden * swish).astype(jnp.bfloat16)
    grad_gpre = (grad_hidden * up_pre * sigmoid * (1.0 + gate_pre * (1.0 - sigmoid))).astype(
        jnp.bfloat16
    )
    grad_wg = across(rows, grad_gpre).astype(jnp.bfloat16)
    grad_wu = across(rows, grad_upre).astype(jnp.bfloat16)
    grad_wd = across(hidden, grads).astype(jnp.bfloat16)
    inputs_grad = (against(grad_gpre, placed_gate) + against(grad_upre, placed_up)).astype(
        jnp.bfloat16
    )
    slots = jnp.einsum(
        "rg,rsd->gsd",
        pick,
        inputs_grad.reshape(capacity, block, depth),
        preferred_element_type=jnp.float32,
    ).astype(jnp.bfloat16)
    returned = lax.all_to_all(slots, "group", split_axis=0, concat_axis=0, tiled=True)
    mine = jnp.einsum("gbk,gsd->bsd", onehot, returned, preferred_element_type=jnp.float32)
    mine = mine.astype(jnp.bfloat16).reshape(shard_rows, depth)
    grad_tokens = jnp.where(live_rows, mine, jnp.zeros((), jnp.bfloat16))
    width = placed_gate.shape[1]
    return (
        grad_tokens,
        grad_wg.reshape(1, depth, width),
        grad_wu.reshape(1, depth, width),
        grad_wd.reshape(1, width, depth),
    )


def solution(mesh):
    return jax.shard_map(
        on_device,
        mesh=mesh,
        in_specs=(
            P(("node", "group"), None),
            P(("node", "group"), None),
            P(("node", "group"), None),
            P(("node", "group")),
            P(("node", "group"), None, None),
            P(),
            P(("node", "group"), None, None),
            P(("node", "group"), None, None),
            P(("node", "group"), None, None),
        ),
        out_specs=(
            P(("node", "group"), None),
            P(("node", "group"), None, None),
            P(("node", "group"), None, None),
            P(("node", "group"), None, None),
        ),
        check_vma=False,
    )
```

profile of v0, /device:TPU:0, one launch (start us, length us, event | category | flops | bytes accessed | tf_op | source)
XLA Modules:
  0.0 169.0 jit_solution(17195871446228643920)
XLA Ops:
  7.9 2.3 %broadcast_select_fusion.5 = (bf16[256,1024]{1,0:T(8,128)(2,1)}, bf16[256,1024]{1,0:T(8,128)(2,1)}) fusion(bf16[256,1024]{1,0:T(8,128)(2,1)} %param.12, pred[256]{0:T(512)(128)(4,1)S(1)} %fusion.16, bf16[256,1024]{1,0:T(8,128)(2,1)} %param.11), kind=kLoop, calls=%fused_computation.35 | loop fusion | flops 524288 | bytes 2097408 | tf_op jit(solution)/shard_map/jit(_where)/select_n | solution.py:65
  10.2 5.2 %all-to-all-start.2 = ((bf16[8,128,256]{2,1,0:T(8,128)(2,1)}), bf16[8,128,256]{2,1,0:T(8,128)(2,1)S(1)}, u32[]{:S(2)}, u32[]{:S(2)}) async-start(bf16[8,128,256]{2,1,0:T(8,128)(2,1)} %bitcast.9), calls=%async_computation.2 | async-start | bytes 1048576 | tf_op jit(solution)/shard_map/all_to_all | solution.py:36
  15.5 0.7 all-gather.5.cloned.1.call-update
  16.2 11.2 %all_gather.12 = s32[4,2,1]{1,2,0:T(1,128)S(1)} all-gather(s32[1,2,1]{1,2,0:T(1,128)S(1)} %copy-done.3), channel_id=1, replica_groups=mesh['node'=8,'group'=4] {'group'}, dimensions={0}, use_global_device_ids=true | all-gather | bytes 40 | tf_op jit(solution)/shard_map/all_gather | solution.py:66
  27.4 0.1 eq.51
  27.5 1.0 sort.17
  28.5 7.8 %all_gather.13 = bf16[1024,1]{0,1:T(2,128)(2,1)S(1)} all-gather(bf16[256,1]{0,1:T(2,128)(2,1)S(1)} %convert_element_type.68), channel_id=1, replica_groups=mesh['node'=8,'group'=4] {'group'}, dimensions={0}, use_global_device_ids=true | all-gather | bytes 2560 | tf_op jit(solution)/shard_map/all_gather | solution.py:83
  36.3 0.6 gather_fusion
  36.9 0.5 compare_and_fusion.1
  37.5 4.1 %all-to-all-start.4 = ((bf16[8,128,256]{2,1,0:T(8,128)(2,1)}), bf16[8,128,256]{2,1,0:T(8,128)(2,1)S(1)}, u32[]{:S(2)}, u32[]{:S(2)}) async-start(bf16[8,128,256]{2,1,0:T(8,128)(2,1)} %bitcast.11), calls=%async_computation.4 | async-start | bytes 1048576 | tf_op jit(solution)/shard_map/all_to_all | solution.py:35
  41.6 3.9 %while.3 = (s32[]{:T(128)}, f32[1024,1]{0,1:T(1,128)S(1)}, s32[3,2]{0,1:T(2,128)S(1)}, f32[3,128,1]{1,2,0:T(1,128)S(1)}, s32[]{:T(128)}) while((s32[]{:T(128)}, f32[1024,1]{0,1:T(1,128)S(1)}, s32[3,2]{0,1:T(2,128)S(1)}, f32[3,128,1]{1,2,0:T(1,128)S(1)}, s32[]{:T(128)}) %tuple.51), condition=%wide.while_cond, body=%wide.while_body.sunk | while | flops 2 | bytes 1129 | solution.py:94
  41.7 0.5 slice.52
  42.2 0.7 constant_dynamic-update-slice_fusion.2
  43.0 0.5 slice.52
  43.5 0.7 constant_dynamic-update-slice_fusion.2
  44.3 0.5 slice.52
  44.8 0.7 constant_dynamic-update-slice_fusion.2
  45.6 5.8 %all-to-all-done.4 = bf16[8,128,256]{2,1,0:T(8,128)(2,1)S(1)} async-done(((bf16[8,128,256]{2,1,0:T(8,128)(2,1)}), bf16[8,128,256]{2,1,0:T(8,128)(2,1)S(1)}, u32[]{:S(2)}, u32[]{:S(2)}) %all-to-all-start.4) | async-done | bytes 524320 | tf_op jit(solution)/shard_map/all_to_all | solution.py:35
  51.4 3.5 %all-to-all-start = ((bf16[8,32,1024]{2,1,0:T(8,128)(2,1)}), bf16[8,32,1024]{2,1,0:T(8,128)(2,1)S(1)}, u32[]{:S(2)}, u32[]{:S(2)}) async-start(bf16[8,32,1024]{2,1,0:T(8,128)(2,1)} %bitcast.6), calls=%async_computation | async-start | bytes 1048576 | tf_op jit(solution)/shard_map/all_to_all | solution.py:37
  54.9 0.6 gather_fusion.2
  55.5 0.6 gather_fusion.3
  56.1 1.1 broadcast_select_fusion.2
  57.2 7.4 %all-to-all-done = bf16[8,32,1024]{2,1,0:T(8,128)(2,1)S(1)} async-done(((bf16[8,32,1024]{2,1,0:T(8,128)(2,1)}), bf16[8,32,1024]{2,1,0:T(8,128)(2,1)S(1)}, u32[]{:S(2)}, u32[]{:S(2)}) %all-to-all-start) | async-done | bytes 524320 | tf_op jit(solution)/shard_map/all_to_all | solution.py:37
  64.5 3.5 %all-to-all-start.5 = ((bf16[8,128,256]{2,1,0:T(8,128)(2,1)}), bf16[8,128,256]{2,1,0:T(8,128)(2,1)S(1)}, u32[]{:S(2)}, u32[]{:S(2)}) async-start(bf16[8,128,256]{2,1,0:T(8,128)(2,1)} %get-tuple-element.63), calls=%async_computation.5 | async-start | bytes 1048576 | tf_op jit(solution)/shard_map/all_to_all | solution.py:43
  68.0 0.6 gather_fusion.1
  68.6 0.9 broadcast_select_fusion.3
  69.6 0.1 broadcast.260.clone
  69.6 6.8 %while.4 = (s32[]{:T(128)}, bf16[1024,1024]{1,0:T(8,128)(2,1)}, s32[3,2]{0,1:T(2,128)S(1)}, bf16[3,128,1024]{2,1,0:T(8,128)(2,1)S(1)}, s32[]{:T(128)}) while((s32[]{:T(128)}, bf16[1024,1024]{1,0:T(8,128)(2,1)}, s32[3,2]{0,1:T(2,128)S(1)}, bf16[3,128,1024]{2,1,0:T(8,128)(2,1)S(1)}, s32[]{:T(128)}) %tuple.64), condition=%wide.while_cond.1, body=%wide.while_body.1.sunk | while | flops 2 | bytes 524393 | solution.py:93
  69.7 0.5 slice.53
  70.3 1.7 bitcast_dynamic-update-slice_fusion.4
  72.0 0.5 slice.53
  72.5 1.7 bitcast_dynamic-update-slice_fusion.4
  74.3 0.5 slice.53
  74.8 1.7 bitcast_dynamic-update-slice_fusion.4
  76.5 1.2 all-to-all-done.5
  77.7 3.5 %all-to-all-start.3 = ((bf16[8,128,256]{2,1,0:T(8,128)(2,1)}), bf16[8,128,256]{2,1,0:T(8,128)(2,1)S(1)}, u32[]{:S(2)}, u32[]{:S(2)}) async-start(bf16[8,128,256]{2,1,0:T(8,128)(2,1)} %get-tuple-element.62), calls=%async_computation.3 | async-start | bytes 1048576 | tf_op jit(solution)/shard_map/all_to_all | solution.py:44
  81.2 24.7 %all-gather.5.cloned.1.call-done = bf16[1024,1024]{1,0:T(8,128)(2,1)} async-done(((bf16[256,1024]{1,0:T(8,128)(2,1)}), bf16[1024,1024]{1,0:T(8,128)(2,1)}) %all-gather.5.cloned.1.call-update) | async-done | bytes 2097168 | tf_op jit(solution)/shard_map/all_gather | solution.py:81
  106.0 6.8 %while.5 = (s32[]{:T(128)}, bf16[1024,1024]{1,0:T(8,128)(2,1)}, s32[3,2]{0,1:T(2,128)S(1)}, bf16[3,128,1024]{2,1,0:T(8,128)(2,1)S(1)}, s32[]{:T(128)}) while((s32[]{:T(128)}, bf16[1024,1024]{1,0:T(8,128)(2,1)}, s32[3,2]{0,1:T(2,128)S(1)}, bf16[3,128,1024]{2,1,0:T(8,128)(2,1)S(1)}, s32[]{:T(128)}) %tuple.65), condition=%wide.while_cond.2, body=%wide.while_body.2.sunk | while | flops 2 | bytes 524393 | solution.py:92
  106.1 0.5 slice.54
  106.6 1.7 bitcast_dynamic-update-slice_fusion.5
  108.3 0.5 slice.54
  108.9 1.7 bitcast_dynamic-update-slice_fusion.5
  110.6 0.5 slice.54
  111.1 1.7 bitcast_dynamic-update-slice_fusion.5
  112.8 1.2 fusion.7
  114.0 4.1 %all-to-all-start.1 = ((bf16[8,32,1024]{2,1,0:T(8,128)(2,1)}), bf16[8,32,1024]{2,1,0:T(8,128)(2,1)}, u32[]{:S(2)}, u32[]{:S(2)}) async-start(bf16[8,32,1024]{2,1,0:T(8,128)(2,1)} %broadcast_select_fusion.3), calls=%async_computation.1 | async-start | bytes 1048576 | tf_op jit(solution)/shard_map/all_to_all | solution.py:45
  118.1 1.1 fusion.27
  119.3 1.1 fusion.26
  120.4 7.5 %all-to-all-done.1 = bf16[8,32,1024]{2,1,0:T(8,128)(2,1)} async-done(((bf16[8,32,1024]{2,1,0:T(8,128)(2,1)}), bf16[8,32,1024]{2,1,0:T(8,128)(2,1)}, u32[]{:S(2)}, u32[]{:S(2)}) %all-to-all-start.1) | async-done | bytes 524320 | tf_op jit(solution)/shard_map/all_to_all | solution.py:45
  127.9 1.9 %multiply_convert_fusion.2 = (bf16[384,256]{1,0:T(8,128)(2,1)S(1)}, bf16[384,256]{1,0:T(8,128)(2,1)S(1)}) fusion(f32[384,256]{1,0:T(8,128)} %fusion.27, f32[384,256]{1,0:T(8,128)} %fusion.26, bf16[384,1024]{1,0:T(8,128)(2,1)} %bitcast.86, bf16[256,1024]{1,0:T(8,128)(2,1)} %bitcast.7), kind=kOutput, calls=%fused_computation.37 | convolution fusion | flops 202604544 | bytes 2490368 | tf_op jit(solution)/shard_map/dot_general | solution.py:8
  129.8 0.4 fusion.28
  130.3 0.4 add_convert_fusion
  130.7 0.2 copy-done.5
  130.9 0.8 convolution_convert_fusion
  131.7 1.3 copy.15
  133.0 3.5 %all-to-all-start.6 = ((bf16[4,128,1024]{2,1,0:T(8,128)(2,1)}), bf16[4,128,1024]{2,1,0:T(8,128)(2,1)S(1)}, u32[]{:S(2)}, u32[]{:S(2)}) async-start(bf16[4,128,1024]{2,1,0:T(8,128)(2,1)} %copy.15), calls=%async_computation.6 | async-start | bytes 2097152 | tf_op jit(solution)/shard_map/all_to_all | solution.py:123
  136.6 0.4 fusion.8
  137.0 1.3 fusion.2
  138.3 1.3 fusion.3
  139.6 1.3 fusion.4
  140.9 19.2 %all-to-all-done.6 = bf16[4,128,1024]{2,1,0:T(8,128)(2,1)S(1)} async-done(((bf16[4,128,1024]{2,1,0:T(8,128)(2,1)}), bf16[4,128,1024]{2,1,0:T(8,128)(2,1)S(1)}, u32[]{:S(2)}, u32[]{:S(2)}) %all-to-all-start.6) | async-done | bytes 1048608 | tf_op jit(solution)/shard_map/all_to_all | solution.py:123
  160.1 1.0 convolution_convert_fusion.4
  161.1 0.1 copy.17
  161.2 0.9 bitcast_select_fusion.1
  (46 shorter events, 1.1 us)
Async XLA Ops:
  7.2 62.4 %all-gather.3.cloned.1.call-start = ((), (), s32[]{:S(2)}) async-start(), calls=%async_computation.7 | async-start | bytes 2621440 | tf_op jit(solution)/shard_map/all_gather | solution.py:82
  10.2 6.0 %copy-start.3 = (s32[1,2,1]{1,2,0:T(1,128)S(1)}, s32[1,2,1]{1,2,0:T(1,128)}, u32[]{:S(2)}) copy-start(s32[1,2,1]{1,2,0:T(1,128)} %param.15) | copy-start | bytes 28
  10.2 18.3 %copy-start.2 = (f32[256,1]{0,1:T(1,128)S(1)}, f32[256,1]{0,1:T(1,128)}, u32[]{:S(2)}) copy-start(f32[256,1]{0,1:T(1,128)} %param.13) | copy-start | bytes 3076
  10.2 35.4 %copy-start.6 = (s32[8]{0:T(128)S(1)}, s32[8]{0:T(128)}, u32[]{:S(2)}) copy-start(s32[8]{0:T(128)} %param.16) | copy-start | bytes 100
  10.2 27.3 %all-to-all-start.2 = ((bf16[8,128,256]{2,1,0:T(8,128)(2,1)}), bf16[8,128,256]{2,1,0:T(8,128)(2,1)S(1)}, u32[]{:S(2)}, u32[]{:S(2)}) async-start(bf16[8,128,256]{2,1,0:T(8,128)(2,1)} %bitcast.9), calls=%async_computation.2 | async-start | bytes 1048576 | tf_op jit(solution)/shard_map/all_to_all | solution.py:36
  15.4 90.5 %all-gather.5.cloned.1.call-start = ((), (), s32[]{:S(2)}) async-start(), calls=%async_computation.8 | async-start | bytes 2621440 | tf_op jit(solution)/shard_map/all_gather | solution.py:81
  37.5 13.9 %all-to-all-start.4 = ((bf16[8,128,256]{2,1,0:T(8,128)(2,1)}), bf16[8,128,256]{2,1,0:T(8,128)(2,1)S(1)}, u32[]{:S(2)}, u32[]{:S(2)}) async-start(bf16[8,128,256]{2,1,0:T(8,128)(2,1)} %bitcast.11), calls=%async_computation.4 | async-start | bytes 1048576 | tf_op jit(solution)/shard_map/all_to_all | solution.py:35
  51.4 13.2 %all-to-all-start = ((bf16[8,32,1024]{2,1,0:T(8,128)(2,1)}), bf16[8,32,1024]{2,1,0:T(8,128)(2,1)S(1)}, u32[]{:S(2)}, u32[]{:S(2)}) async-start(bf16[8,32,1024]{2,1,0:T(8,128)(2,1)} %bitcast.6), calls=%async_computation | async-start | bytes 1048576 | tf_op jit(solution)/shard_map/all_to_all | solution.py:37
  64.5 13.2 %all-to-all-start.5 = ((bf16[8,128,256]{2,1,0:T(8,128)(2,1)}), bf16[8,128,256]{2,1,0:T(8,128)(2,1)S(1)}, u32[]{:S(2)}, u32[]{:S(2)}) async-start(bf16[8,128,256]{2,1,0:T(8,128)(2,1)} %get-tuple-element.63), calls=%async_computation.5 | async-start | bytes 1048576 | tf_op jit(solution)/shard_map/all_to_all | solution.py:43
  77.7 36.3 %all-to-all-start.3 = ((bf16[8,128,256]{2,1,0:T(8,128)(2,1)}), bf16[8,128,256]{2,1,0:T(8,128)(2,1)S(1)}, u32[]{:S(2)}, u32[]{:S(2)}) async-start(bf16[8,128,256]{2,1,0:T(8,128)(2,1)} %get-tuple-element.62), calls=%async_computation.3 | async-start | bytes 1048576 | tf_op jit(solution)/shard_map/all_to_all | solution.py:44
  114.0 13.9 %all-to-all-start.1 = ((bf16[8,32,1024]{2,1,0:T(8,128)(2,1)}), bf16[8,32,1024]{2,1,0:T(8,128)(2,1)}, u32[]{:S(2)}, u32[]{:S(2)}) async-start(bf16[8,32,1024]{2,1,0:T(8,128)(2,1)} %broadcast_select_fusion.3), calls=%async_computation.1 | async-start | bytes 1048576 | tf_op jit(solution)/shard_map/all_to_all | solution.py:45
  130.2 0.6 copy-start.5
  133.0 27.1 %all-to-all-start.6 = ((bf16[4,128,1024]{2,1,0:T(8,128)(2,1)}), bf16[4,128,1024]{2,1,0:T(8,128)(2,1)S(1)}, u32[]{:S(2)}, u32[]{:S(2)}) async-start(bf16[4,128,1024]{2,1,0:T(8,128)(2,1)} %copy.15), calls=%async_computation.6 | async-start | bytes 2097152 | tf_op jit(solution)/shard_map/all_to_all | solution.py:123
  137.0 2.6 %copy-start = (f32[384,256]{1,0:T(8,128)S(1)}, f32[384,256]{1,0:T(8,128)}, u32[]{:S(2)}) copy-start(f32[384,256]{1,0:T(8,128)} %fusion.27) | copy-start | bytes 1179652
  137.0 2.6 %copy-start.1 = (f32[384,256]{1,0:T(8,128)S(1)}, f32[384,256]{1,0:T(8,128)}, u32[]{:S(2)}) copy-start(f32[384,256]{1,0:T(8,128)} %fusion.26) | copy-start | bytes 1179652
  139.6 20.6 %copy-start.4 = (s32[1,2,1]{1,2,0:T(1,128)S(1)}, s32[1,2,1]{1,2,0:T(1,128)}, u32[]{:S(2)}) copy-start(s32[1,2,1]{1,2,0:T(1,128)} %param.15) | copy-start | bytes 28
Sparse Core Ops, SparseCore 0:
  10.3 48.6 all-gather.2
  61.2 44.6 all-gather.4
where the time goes:
time: 170 us; the launch traced here: 169 us
  waiting for transfers between devices  66.5 us (39%)
  starting transfers between devices  27.5 us (16%)
  local copies, waits for them, and re-layouts  21.9 us (13%)
  blocking collectives  19 us (11%)
  between operations  14.9 us (9%)
  matrix products  10.6 us (6%)
  other arithmetic  8.42 us (5%)
    all_gather x1, waiting for transfers between devices, on_device(): tok_piece = lax.all_gather(masked_tok, 'group', axis=0, tiled=True)  24.7 us
    all_to_all x1, waiting for transfers between devices, on_device(): lax.all_to_all(slots, 'group', split_axis=0, concat_axis=0, tiled=True)  19.2 us
    gather x27, local copies, waits for them, and re-layouts  17.5 us
    all_gather x1, blocking collectives, on_device(): table = lax.all_gather(routes, 'group', axis=0, tiled=True)  11.2 us
    all_gather x1, blocking collectives, on_device(): lax.all_gather(router_gate.astype(jnp.bfloat16), 'group', axis=0, tiled=T...  7.78 us
    all_to_all x1, waiting for transfers between devices, relocate(): lax.all_to_all(down_pick, 'node', split_axis=0, concat_axis=0, tiled=True)  7.52 us
    all_to_all x1, waiting for transfers between devices, relocate(): lax.all_to_all(down_parts, 'node', split_axis=0, concat_axis=0, tiled=True)  7.36 us
    all_to_all x1, waiting for transfers between devices, relocate(): lax.all_to_all(gate_parts, 'node', split_axis=0, concat_axis=0, tiled=True)  5.78 us
  transfers between devices with their start and end apart: 9, of which 6 were waited for; matrix products, arithmetic and copies ran while one was open for 19% of the time, Pallas kernels for 0%

commit v1 on v0

v1 whole, which is shorter than its diff:
```python
import functools

import jax
import jax.numpy as jnp
from jax import lax
from jax.experimental import pallas as pl
from jax.experimental.pallas import tpu as pltpu
from jax.sharding import PartitionSpec as P

VMEM = pltpu.VMEM
SMEM = pltpu.SMEM
LIMIT = 48 * 1024 * 1024


def dot(left, right, dims):
    return lax.dot_general(left, right, (dims, ((), ())), preferred_element_type=jnp.float32)


def params():
    return pltpu.CompilerParams(vmem_limit_bytes=LIMIT)


def spec(space):
    return pl.BlockSpec(memory_space=space)


def pack_kernel(hops, counts, routes, tokens, grad_out, gate, *places):
    slots, topk = routes.shape[1], routes.shape[2]
    block = tokens.shape[0] // slots
    me = lax.axis_index("group")
    for hop, place in zip(hops, places):
        place[...] = jnp.zeros_like(place)
        for b in range(slots):
            rows = pl.ds(b * block, block)
            for k in range(topk):

                @pl.when((routes[0, b, k] == hop(me)) & (b < counts[0]))
                def _():
                    place[:block] = tokens[rows]
                    scaled = gate[rows, k : k + 1] * grad_out[rows].astype(jnp.float32)
                    place[block:] = scaled.astype(jnp.bfloat16)


def pack(hops, counts, routes, tokens, grad_out, gate):
    slots = routes.shape[1]
    block, depth = tokens.shape[0] // slots, tokens.shape[1]
    place = jax.ShapeDtypeStruct((2 * block, depth), jnp.bfloat16)
    return pl.pallas_call(
        functools.partial(pack_kernel, hops),
        out_shape=[place] * len(hops),
        in_specs=[spec(SMEM), spec(SMEM), spec(VMEM), spec(VMEM), spec(VMEM)],
        out_specs=[spec(VMEM)] * len(hops),
        compiler_params=params(),
        name="pack",
    )(counts, routes, tokens, grad_out, gate)


def expert_kernel(place, w_gate, w_up, w_down, back, inner):
    block = place.shape[0] // 2
    rows, grads = place[:block], place[block:]
    gate_w, up_w = w_gate[...], w_up[...]
    gate_pre = dot(rows, gate_w, ((1,), (0,)))
    up_pre = dot(rows, up_w, ((1,), (0,)))
    sig = 1.0 / (1.0 + jnp.exp(-gate_pre))
    swish = gate_pre * sig
    grad_hidden = dot(grads, w_down[...], ((1,), (1,)))
    grad_upre = (grad_hidden * swish).astype(jnp.bfloat16)
    grad_gpre = (grad_hidden * up_pre * sig * (1.0 + gate_pre * (1.0 - sig))).astype(jnp.bfloat16)
    back[...] = (dot(grad_gpre, gate_w, ((1,), (1,))) + dot(grad_upre, up_w, ((1,), (1,)))).astype(jnp.bfloat16)
    inner[0] = grad_gpre
    inner[1] = grad_upre
    inner[2] = (swish * up_pre).astype(jnp.bfloat16)


def expert(place, w_gate, w_up, w_down):
    block, depth = place.shape[0] // 2, place.shape[1]
    width = w_gate.shape[1]
    return pl.pallas_call(
        expert_kernel,
        out_shape=[
            jax.ShapeDtypeStruct((block, depth), jnp.bfloat16),
            jax.ShapeDtypeStruct((3, block, width), jnp.bfloat16),
        ],
        in_specs=[spec(VMEM)] * 4,
        out_specs=[spec(VMEM)] * 2,
        compiler_params=params(),
        cost_estimate=pl.CostEstimate(
            flops=10 * block * depth * width, bytes_accessed=8 * depth * width, transcendentals=block * width
        ),
        name="expert",
    )(place, w_gate, w_up, w_down)


def weights_kernel(count, *refs):
    places, inners = refs[:count], refs[count : 2 * count]
    grad_gate, grad_up, grad_down = refs[2 * count :]
    block = places[0].shape[0] // 2
    rows = jnp.concatenate([place[:block] for place in places], axis=0)
    grads = jnp.concatenate([place[block:] for place in places], axis=0)
    gpre, upre, hidden = (jnp.concatenate([inner[i] for inner in inners], axis=0) for i in range(3))
    grad_gate[0] = dot(rows, gpre, ((0,), (0,))).astype(jnp.bfloat16)
    grad_up[0] = dot(rows, upre, ((0,), (0,))).astype(jnp.bfloat16)
    grad_down[0] = dot(hidden, grads, ((0,), (0,))).astype(jnp.bfloat16)


def weights(places, inners):
    count = len(places)
    block, depth = places[0].shape[0] // 2, places[0].shape[1]
    width = inners[0].shape[2]
    tile = min(depth, 256)
    wide = jax.ShapeDtypeStruct((1, depth, width), jnp.bfloat16)
    tall = jax.ShapeDtypeStruct((1, width, depth), jnp.bfloat16)
    return pl.pallas_call(
        functools.partial(weights_kernel, count),
        out_shape=[wide, wide, tall],
        grid=(depth // tile,),
        in_specs=[pl.BlockSpec((2 * block, tile), lambda i: (0, i))] * count
        + [pl.BlockSpec((3, block, width), lambda i: (0, 0, 0))] * count,
        out_specs=[
            pl.BlockSpec((1, tile, width), lambda i: (0, i, 0)),
            pl.BlockSpec((1, tile, width), lambda i: (0, i, 0)),
            pl.BlockSpec((1, width, tile), lambda i: (0, 0, i)),
        ],
        compiler_params=params(),
        cost_estimate=pl.CostEstimate(
            flops=6 * count * block * depth * width, bytes_accessed=10 * depth * width, transcendentals=0
        ),
        name="weight_grads",
    )(*places, *inners)


def combine_kernel(hops, counts, routes, *refs):
    returned, out, total = refs[: len(hops)], refs[len(hops)], refs[len(hops) + 1]
    slots, topk = routes.shape[1], routes.shape[2]
    block = out.shape[0] // slots
    me = lax.axis_index("group")
    for b in range(slots):
        total[...] = jnp.zeros_like(total)
        for k in range(topk):
            for hop, part in zip(hops, returned):

                @pl.when((routes[0, b, k] == hop(me)) & (b < counts[0]))
                def _():
                    total[...] += part[...].astype(jnp.float32)

        out[b * block : (b + 1) * block] = total[...].astype(jnp.bfloat16)


def combine(hops, counts, routes, returned):
    slots = routes.shape[1]
    block, depth = returned[0].shape
    return pl.pallas_call(
        functools.partial(combine_kernel, hops),
        out_shape=jax.ShapeDtypeStruct((slots * block, depth), jnp.bfloat16),
        in_specs=[spec(SMEM), spec(SMEM)] + [spec(VMEM)] * len(hops),
        out_specs=spec(VMEM),
        scratch_shapes=[VMEM((block, depth), jnp.float32)],
        compiler_params=params(),
        name="combine",
    )(counts, routes, *returned)


def xor_pairs(size, d):
    return [(i, i ^ d) for i in range(size)]


def relocate(partner, arrays):
    nodes = lax.axis_size("node")
    distance = lax.axis_index("node") ^ partner[lax.axis_index("node")]

    def branch(d):
        return lambda *held: tuple(lax.ppermute(a, "node", xor_pairs(nodes, d)) for a in held)

    return lax.switch(distance - 1, [branch(d) for d in range(1, nodes)], *arrays)


def on_device(tokens, grad_out, router_gate, counts, routes, partner, w_gate, w_up, w_down):
    group = lax.axis_size("group")
    order = sorted(range(1, group), key=lambda d: (d != 2, -d)) + [0]
    hops = [functools.partial(lambda d, me: me ^ d, d) for d in order]
    packed = pack(hops, counts, routes, tokens, grad_out, router_gate)
    places = [
        lax.ppermute(place, "group", xor_pairs(group, d)) if d else place for d, place in zip(order, packed)
    ]
    placed = relocate(partner, (w_gate[0], w_up[0], w_down[0]))
    results = [expert(place, *placed) for place in places]
    returned = [
        lax.ppermute(back, "group", xor_pairs(group, d)) if d else back for d, (back, _) in zip(order, results)
    ]
    grads = weights(places, [inner for _, inner in results])
    grad_tokens = combine(hops, counts, routes, returned)
    return (grad_tokens, *grads)


def solution(mesh):
    both = ("node", "group")
    rows = P(both, None)
    cube = P(both, None, None)
    return jax.shard_map(
        on_device,
        mesh=mesh,
        in_specs=(rows, rows, rows, P(both), cube, P(), cube, cube, cube),
        out_specs=(rows, cube, cube, cube),
        check_vma=False,
    )
```

time: 170 us -> 82.5 us (0.49)
  waiting for transfers between devices: 66.5 us -> 32.8 us
  blocking collectives: 19 us -> 0 us
  local copies, waits for them, and re-layouts: 21.9 us -> 4.13 us
  Pallas kernels: 0 us -> 15.1 us
  between operations: 14.9 us -> 2.05 us
  matrix products: 10.6 us -> 0 us
  other arithmetic: 8.42 us -> 0 us
    all_to_all x7 -> x0, waiting for transfers between devices: 41.1 us -> none  [the longest x1 19.2 us: on_device(): lax.all_to_all(slots, 'group', split_axis=0, concat_axis=0, tiled=True)]
    ppermute x0 -> x9, waiting for transfers between devices: none -> 32.8 us  [the longest x3 18 us: branch(): lax.ppermute(a, 'node', xor_pairs(nodes, d))]
    ppermute x0 -> x9, starting transfers between devices: none -> 28 us  [the longest x3 20 us: on_device(): lax.ppermute(back, 'group', xor_pairs(group, d))]
    all_to_all x7 -> x0, starting transfers between devices: 27.5 us -> none  [the longest x1 5.2 us: relocate(): lax.all_to_all(up_parts, 'node', split_axis=0, concat_axis=0, tiled=True)]
    all_gather x2 -> x0, waiting for transfers between devices: 24.7 us -> none  [the longest x1 24.7 us: on_device(): tok_piece = lax.all_gather(masked_tok, 'group', axis=0, tiled=True)]
    gather x31 -> x0, local copies, waits for them, and re-layouts: 19.9 us -> none
    all_gather x2 -> x0, blocking collectives: 19 us -> none  [the longest x1 11.2 us: on_device(): table = lax.all_gather(routes, 'group', axis=0, tiled=True)]
    pallas_call x0 -> x7, Pallas kernels: none -> 15.1 us  [the longest x4 9.78 us: expert(): pl.pallas_call(expert_kernel, out_shape=[jax.ShapeDtypeStruct((block, dep...]
  transfers between devices with their start and end apart: 9 -> 9, of which waited for: 6 -> 6; matrix products, arithmetic and copies ran while one was open for 19% -> 1% of each run, Pallas kernels for 0% -> 15%
where the time goes in v1:
time: 82.5 us; the launch traced here: 82.1 us
  waiting for transfers between devices  32.8 us (40%)
  starting transfers between devices  28 us (34%)
  Pallas kernels  15.1 us (18%)
  local copies, waits for them, and re-layouts  4.13 us (5%)
  between operations  2.05 us (2%)
    ppermute x3, starting transfers between devices, on_device(): lax.ppermute(back, 'group', xor_pairs(group, d))  20 us
    ppermute x3, waiting for transfers between devices, branch(): lax.ppermute(a, 'node', xor_pairs(nodes, d))  18 us
    ppermute x3, waiting for transfers between devices, on_device(): lax.ppermute(place, 'group', xor_pairs(group, d))  14.1 us
    pallas_call x4, Pallas kernels, expert(): pl.pallas_call(expert_kernel, out_shape=[jax.ShapeDtypeStruct((block, dep...  9.78 us
    ppermute x3, starting transfers between devices, on_device(): lax.ppermute(place, 'group', xor_pairs(group, d))  5.79 us
    unnamed x12, local copies, waits for them, and re-layouts  3.54 us
    pallas_call x1, Pallas kernels, weights(): pl.pallas_call(functools.partial(weights_kernel, count), out_shape=[wide,...  2.9 us
    ppermute x3, starting transfers between devices, branch(): lax.ppermute(a, 'node', xor_pairs(nodes, d))  2.23 us
  transfers between devices with their start and end apart: 9, of which 6 were waited for; matrix products, arithmetic and copies ran while one was open for 1% of the time, Pallas kernels for 15%

profile of v1, /device:TPU:0, one launch (start us, length us, event | category | flops | bytes accessed | tf_op | source)
XLA Modules:
  0.0 82.1 jit_solution(6706484424507978311)
XLA Ops:
  0.6 0.0 copy-start.3
  1.3 0.0 copy-done.3
  1.3 0.0 copy-start.2
  1.3 0.1 copy.15.routes
  1.4 0.6 copy-done.2
  2.0 0.1 copy.14.gate
  2.1 0.0 copy-start
  2.1 1.0 %copy-done = bf16[256,1024]{1,0:T(8,128)(2,1)S(1)} copy-done((bf16[256,1024]{1,0:T(8,128)(2,1)S(1)}, bf16[256,1024]{1,0:T(8,128)(2,1)}, u32[]{:S(2)}) %copy-start) | copy-done | bytes 524312
  3.2 0.0 copy-start.1
  3.2 1.0 %copy-done.1 = bf16[256,1024]{1,0:T(8,128)(2,1)S(1)} copy-done((bf16[256,1024]{1,0:T(8,128)(2,1)S(1)}, bf16[256,1024]{1,0:T(8,128)(2,1)}, u32[]{:S(2)}) %copy-start.1) | copy-done | bytes 524312
  4.2 0.8 %pack.1 = (bf16[256,1024]{1,0:T(8,128)(2,1)S(1)}, bf16[256,1024]{1,0:T(8,128)(2,1)S(1)}, bf16[256,1024]{1,0:T(8,128)(2,1)S(1)}, bf16[256,1024]{1,0:T(8,128)(2,1)S(1)}) custom-call(s32[1]{0:T(128)S(6)} %copy.37.counts, s32[1,2,1]{2,1,0:T(2,128)S(1)} %copy.15.routes, bf16[256,1024]{1,0:T(8,128)(2,1)S(1)} %copy-done, bf16[256,1024]{1,0:T(8,128)(2,1)S(1)} %copy-done.1, ...), custom_call_target="tpu_custom_call" | custom-call | tf_op jit(solution)/shard_map/pack/pallas_call | solution.py:48
  5.1 4.2 %collective-permute-start.21 = (bf16[256,1024]{1,0:T(8,128)(2,1)S(1)}, bf16[256,1024]{1,0:T(8,128)(2,1)S(1)}, u32[]{:S(2)}, u32[]{:S(2)}) collective-permute-start(bf16[256,1024]{1,0:T(8,128)(2,1)S(1)} %get-tuple-element.85), channel_id=1, source_target_pairs={{0,2},{1,3},{2,0},{3,1},{4,6},{5,7},{6,4},{7,5},{8,10},{9,11},{10,... | collective-permute-start | bytes 1572872 | tf_op jit(solution)/shard_map/ppermute | solution.py:183
  9.3 1.3 %collective-permute-start.23 = (bf16[256,1024]{1,0:T(8,128)(2,1)S(1)}, bf16[256,1024]{1,0:T(8,128)(2,1)S(1)}, u32[]{:S(2)}, u32[]{:S(2)}) collective-permute-start(bf16[256,1024]{1,0:T(8,128)(2,1)S(1)} %get-tuple-element.90), channel_id=1, source_target_pairs={{0,3},{1,2},{2,1},{3,0},{4,7},{5,6},{6,5},{7,4},{8,11},{9,10},{10,... | collective-permute-start | bytes 1572872 | tf_op jit(solution)/shard_map/ppermute | solution.py:183
  10.6 0.0 copy-start.4
  10.6 0.7 copy-done.4
  11.3 0.6 dynamic_slice.3
  12.5 20.2 %conditional.1 = (bf16[1024,256]{1,0:T(8,128)(2,1)}, bf16[1024,256]{1,0:T(8,128)(2,1)}, bf16[256,1024]{1,0:T(8,128)(2,1)}) conditional(s32[]{:T(128)} %clamp.3, (bf16[1024,256]{1,0:T(8,128)(2,1)}, bf16[1024,256]{1,0:T(8,128)(2,1)}, bf16[256,1024]{1,0:T(8,128)(2,1)}) %tuple.59, (bf16[1024,256]{1,0:T(8,128)(2,1)}, ...), branch_computations={%region_0.0_spmd, %region_1.0_spmd, %region_2.0_spmd, %region_3.0_... | conditional | bytes 6291600 | solution.py:174
  12.5 0.5 collective-permute-start.12
  13.0 1.3 %collective-permute-start.13 = (bf16[1024,256]{1,0:T(8,128)(2,1)}, bf16[1024,256]{1,0:T(8,128)(2,1)}, u32[]{:S(2)}, u32[]{:S(2)}) collective-permute-start(bf16[1024,256]{1,0:T(8,128)(2,1)} %get-tuple-element.55), channel_id=1, source_target_pairs={{0,20},{4,16},{8,28},{12,24},{16,4},{20,0},{24,12},{28,8},{1,21},{... | collective-permute-start | bytes 1572872 | tf_op jit(solution)/shard_map/cond/branch_4_fun/ppermute | solution.py:172
  14.3 0.4 collective-permute-start.14
  14.8 6.8 %collective-permute-done.12 = bf16[1024,256]{1,0:T(8,128)(2,1)} collective-permute-done((bf16[1024,256]{1,0:T(8,128)(2,1)}, bf16[1024,256]{1,0:T(8,128)(2,1)}, u32[]{:S(2)}, u32[]{:S(2)}) %collective-permute-start.12) | collective-permute-done | bytes 524320 | tf_op jit(solution)/shard_map/cond/branch_4_fun/ppermute | solution.py:172
  21.5 5.6 %collective-permute-done.13 = bf16[1024,256]{1,0:T(8,128)(2,1)} collective-permute-done((bf16[1024,256]{1,0:T(8,128)(2,1)}, bf16[1024,256]{1,0:T(8,128)(2,1)}, u32[]{:S(2)}, u32[]{:S(2)}) %collective-permute-start.13) | collective-permute-done | bytes 524320 | tf_op jit(solution)/shard_map/cond/branch_4_fun/ppermute | solution.py:172
  27.1 5.6 %collective-permute-done.14 = bf16[256,1024]{1,0:T(8,128)(2,1)} collective-permute-done((bf16[256,1024]{1,0:T(8,128)(2,1)}, bf16[256,1024]{1,0:T(8,128)(2,1)}, u32[]{:S(2)}, u32[]{:S(2)}) %collective-permute-start.14) | collective-permute-done | bytes 524320 | tf_op jit(solution)/shard_map/cond/branch_4_fun/ppermute | solution.py:172
  32.8 0.2 collective-permute-start.25
  33.0 11.6 %collective-permute-done.21.place.refs_0_ = bf16[256,1024]{1,0:T(8,128)(2,1)S(1)} collective-permute-done((bf16[256,1024]{1,0:T(8,128)(2,1)S(1)}, bf16[256,1024]{1,0:T(8,128)(2,1)S(1)}, u32[]{:S(2)}, u32[]{:S(2)}) %collective-permute-start.21) | collective-permute-done | bytes 524320 | tf_op jit(solution)/shard_map/ppermute | solution.py:183
  44.6 2.4 %expert.4 = (bf16[128,1024]{1,0:T(8,128)(2,1)S(1)}, bf16[3,128,256]{2,1,0:T(8,128)(2,1)S(1)}) custom-call(bf16[256,1024]{1,0:T(8,128)(2,1)S(1)} %collective-permute-done.21.place.refs_0_, bf16[1024,256]{1,0:T(8,128)(2,1)} %get-tuple-element.86.w_gate, bf16[1024,256]{1,0:T(8,128)(2,1)} %get-tuple-element.87.w_up, bf16[256,1024]{1,0:T(8,128)(2,1)} %get-tuple-element.88.w_down), custom_call_target="tpu_custom_call" | custom-call | flops 335544320 | bytes 2097152 | tf_op jit(solution)/shard_map/expert/pallas_call | solution.py:78
  47.0 0.1 collective-permute-start.22
  47.1 0.0 collective-permute-done.23.place.refs_1_
  47.1 2.4 %expert.5 = (bf16[128,1024]{1,0:T(8,128)(2,1)S(1)}, bf16[3,128,256]{2,1,0:T(8,128)(2,1)S(1)}) custom-call(bf16[256,1024]{1,0:T(8,128)(2,1)S(1)} %collective-permute-done.23.place.refs_1_, bf16[1024,256]{1,0:T(8,128)(2,1)} %get-tuple-element.86.w_gate, bf16[1024,256]{1,0:T(8,128)(2,1)} %get-tuple-element.87.w_up, bf16[256,1024]{1,0:T(8,128)(2,1)} %get-tuple-element.88.w_down), custom_call_target="tpu_custom_call" | custom-call | flops 335544320 | bytes 2097152 | tf_op jit(solution)/shard_map/expert/pallas_call | solution.py:78
  49.5 2.7 %collective-permute-start.24 = (bf16[128,1024]{1,0:T(8,128)(2,1)S(1)}, bf16[128,1024]{1,0:T(8,128)(2,1)S(1)}, u32[]{:S(2)}, u32[]{:S(2)}) collective-permute-start(bf16[128,1024]{1,0:T(8,128)(2,1)S(1)} %get-tuple-element.91), channel_id=1, source_target_pairs={{0,3},{1,2},{2,1},{3,0},{4,7},{5,6},{6,5},{7,4},{8,11},{9,10},{10,... | collective-permute-start | bytes 786440 | tf_op jit(solution)/shard_map/ppermute | solution.py:188
  52.3 2.5 %collective-permute-done.25.place.refs_2_ = bf16[256,1024]{1,0:T(8,128)(2,1)S(1)} collective-permute-done((bf16[256,1024]{1,0:T(8,128)(2,1)S(1)}, bf16[256,1024]{1,0:T(8,128)(2,1)S(1)}, u32[]{:S(2)}, u32[]{:S(2)}) %collective-permute-start.25) | collective-permute-done | bytes 524320 | tf_op jit(solution)/shard_map/ppermute | solution.py:183
  54.8 2.4 %expert.6 = (bf16[128,1024]{1,0:T(8,128)(2,1)S(1)}, bf16[3,128,256]{2,1,0:T(8,128)(2,1)S(1)}) custom-call(bf16[256,1024]{1,0:T(8,128)(2,1)S(1)} %collective-permute-done.25.place.refs_2_, bf16[1024,256]{1,0:T(8,128)(2,1)} %get-tuple-element.86.w_gate, bf16[1024,256]{1,0:T(8,128)(2,1)} %get-tuple-element.87.w_up, bf16[256,1024]{1,0:T(8,128)(2,1)} %get-tuple-element.88.w_down), custom_call_target="tpu_custom_call" | custom-call | flops 335544320 | bytes 2097152 | tf_op jit(solution)/shard_map/expert/pallas_call | solution.py:78
  57.2 17.1 %collective-permute-start.26 = (bf16[128,1024]{1,0:T(8,128)(2,1)S(1)}, bf16[128,1024]{1,0:T(8,128)(2,1)S(1)}, u32[]{:S(2)}, u32[]{:S(2)}) collective-permute-start(bf16[128,1024]{1,0:T(8,128)(2,1)S(1)} %get-tuple-element.93), channel_id=1, source_target_pairs={{0,1},{1,0},{2,3},{3,2},{4,5},{5,4},{6,7},{7,6},{8,9},{9,8},{10,11... | collective-permute-start | bytes 786440 | tf_op jit(solution)/shard_map/ppermute | solution.py:188
  74.4 2.4 %expert.7 = (bf16[128,1024]{1,0:T(8,128)(2,1)S(1)}, bf16[3,128,256]{2,1,0:T(8,128)(2,1)S(1)}) custom-call(bf16[256,1024]{1,0:T(8,128)(2,1)S(1)} %get-tuple-element.94.place.refs_3_, bf16[1024,256]{1,0:T(8,128)(2,1)} %get-tuple-element.86.w_gate, bf16[1024,256]{1,0:T(8,128)(2,1)} %get-tuple-element.87.w_up, bf16[256,1024]{1,0:T(8,128)(2,1)} %get-tuple-element.88.w_down), custom_call_target="tpu_custom_call" | custom-call | flops 335544320 | bytes 2097152 | tf_op jit(solution)/shard_map/expert/pallas_call | solution.py:78
  76.8 2.9 %weight_grads.1 = (bf16[1,1024,256]{2,1,0:T(8,128)(2,1)}, bf16[1,1024,256]{2,1,0:T(8,128)(2,1)}, bf16[1,256,1024]{2,1,0:T(8,128)(2,1)}) custom-call(bf16[256,1024]{1,0:T(8,128)(2,1)S(1)} %collective-permute-done.21.place.refs_0_, bf16[256,1024]{1,0:T(8,128)(2,1)S(1)} %collective-permute-done.23.place.refs_1_, ...), custom_call_target="tpu_custom_call" | custom-call | flops 805306368 | bytes 2621440 | tf_op jit(solution)/shard_map/weight_grads/pallas_call | solution.py:113
  79.7 0.0 collective-permute-done.22.refs_0_
  79.8 0.0 collective-permute-done.24.refs_1_
  79.8 0.8 collective-permute-done.26.refs_2_
  80.5 1.6 %combine.1 = bf16[256,1024]{1,0:T(8,128)(2,1)} custom-call(s32[1]{0:T(128)S(6)} %copy.37.counts, s32[1,2,1]{2,1,0:T(2,128)S(1)} %copy.15.routes, bf16[128,1024]{1,0:T(8,128)(2,1)S(1)} %collective-permute-done.22.refs_0_, bf16[128,1024]{1,0:T(8,128)(2,1)S(1)} %collective-permute-done.24.refs_1_, bf16[128,1024]{1,0:T(8,128)(2,1)S(1)} %collective-permute-done.26.refs_2_, ...), custom_call_target="tpu_custom_call" | custom-call | tf_op jit(solution)/shard_map/combine/pallas_call | solution.py:152
Async XLA Ops:
  0.6 0.7 copy-start.3
  1.3 0.7 copy-start.2
  2.1 1.0 %copy-start = (bf16[256,1024]{1,0:T(8,128)(2,1)S(1)}, bf16[256,1024]{1,0:T(8,128)(2,1)}, u32[]{:S(2)}) copy-start(bf16[256,1024]{1,0:T(8,128)(2,1)} %tokens.1) | copy-start | bytes 1572868
  3.2 1.0 %copy-start.1 = (bf16[256,1024]{1,0:T(8,128)(2,1)S(1)}, bf16[256,1024]{1,0:T(8,128)(2,1)}, u32[]{:S(2)}) copy-start(bf16[256,1024]{1,0:T(8,128)(2,1)} %grad_out.1) | copy-start | bytes 1572868
  5.1 39.5 %collective-permute-start.21 = (bf16[256,1024]{1,0:T(8,128)(2,1)S(1)}, bf16[256,1024]{1,0:T(8,128)(2,1)S(1)}, u32[]{:S(2)}, u32[]{:S(2)}) collective-permute-start(bf16[256,1024]{1,0:T(8,128)(2,1)S(1)} %get-tuple-element.85), channel_id=1, source_target_pairs={{0,2},{1,3},{2,0},{3,1},{4,6},{5,7},{6,4},{7,5},{8,10},{9,11},{10,... | collective-permute-start | bytes 1572872 | tf_op jit(solution)/shard_map/ppermute | solution.py:183
  9.3 37.8 %collective-permute-start.23 = (bf16[256,1024]{1,0:T(8,128)(2,1)S(1)}, bf16[256,1024]{1,0:T(8,128)(2,1)S(1)}, u32[]{:S(2)}, u32[]{:S(2)}) collective-permute-start(bf16[256,1024]{1,0:T(8,128)(2,1)S(1)} %get-tuple-element.90), channel_id=1, source_target_pairs={{0,3},{1,2},{2,1},{3,0},{4,7},{5,6},{6,5},{7,4},{8,11},{9,10},{10,... | collective-permute-start | bytes 1572872 | tf_op jit(solution)/shard_map/ppermute | solution.py:183
  10.6 0.7 copy-start.4
  12.5 9.0 %collective-permute-start.12 = (bf16[1024,256]{1,0:T(8,128)(2,1)}, bf16[1024,256]{1,0:T(8,128)(2,1)}, u32[]{:S(2)}, u32[]{:S(2)}) collective-permute-start(bf16[1024,256]{1,0:T(8,128)(2,1)} %get-tuple-element.54), channel_id=1, source_target_pairs={{0,20},{4,16},{8,28},{12,24},{16,4},{20,0},{24,12},{28,8},{1,21},{... | collective-permute-start | bytes 1572872 | tf_op jit(solution)/shard_map/cond/branch_4_fun/ppermute | solution.py:172
  13.0 14.1 %collective-permute-start.13 = (bf16[1024,256]{1,0:T(8,128)(2,1)}, bf16[1024,256]{1,0:T(8,128)(2,1)}, u32[]{:S(2)}, u32[]{:S(2)}) collective-permute-start(bf16[1024,256]{1,0:T(8,128)(2,1)} %get-tuple-element.55), channel_id=1, source_target_pairs={{0,20},{4,16},{8,28},{12,24},{16,4},{20,0},{24,12},{28,8},{1,21},{... | collective-permute-start | bytes 1572872 | tf_op jit(solution)/shard_map/cond/branch_4_fun/ppermute | solution.py:172
  14.3 18.4 %collective-permute-start.14 = (bf16[256,1024]{1,0:T(8,128)(2,1)}, bf16[256,1024]{1,0:T(8,128)(2,1)}, u32[]{:S(2)}, u32[]{:S(2)}) collective-permute-start(bf16[256,1024]{1,0:T(8,128)(2,1)} %get-tuple-element.56), channel_id=1, source_target_pairs={{0,20},{4,16},{8,28},{12,24},{16,4},{20,0},{24,12},{28,8},{1,21},{... | collective-permute-start | bytes 1572872 | tf_op jit(solution)/shard_map/cond/branch_4_fun/ppermute | solution.py:172
  32.8 22.0 %collective-permute-start.25 = (bf16[256,1024]{1,0:T(8,128)(2,1)S(1)}, bf16[256,1024]{1,0:T(8,128)(2,1)S(1)}, u32[]{:S(2)}, u32[]{:S(2)}) collective-permute-start(bf16[256,1024]{1,0:T(8,128)(2,1)S(1)} %get-tuple-element.92), channel_id=1, source_target_pairs={{0,1},{1,0},{2,3},{3,2},{4,5},{5,4},{6,7},{7,6},{8,9},{9,8},{10,11... | collective-permute-start | bytes 1572872 | tf_op jit(solution)/shard_map/ppermute | solution.py:183
  47.0 32.8 %collective-permute-start.22 = (bf16[128,1024]{1,0:T(8,128)(2,1)S(1)}, bf16[128,1024]{1,0:T(8,128)(2,1)S(1)}, u32[]{:S(2)}, u32[]{:S(2)}) collective-permute-start(bf16[128,1024]{1,0:T(8,128)(2,1)S(1)} %get-tuple-element.89), channel_id=1, source_target_pairs={{0,2},{1,3},{2,0},{3,1},{4,6},{5,7},{6,4},{7,5},{8,10},{9,11},{10,... | collective-permute-start | bytes 786440 | tf_op jit(solution)/shard_map/ppermute | solution.py:188
  49.5 30.2 %collective-permute-start.24 = (bf16[128,1024]{1,0:T(8,128)(2,1)S(1)}, bf16[128,1024]{1,0:T(8,128)(2,1)S(1)}, u32[]{:S(2)}, u32[]{:S(2)}) collective-permute-start(bf16[128,1024]{1,0:T(8,128)(2,1)S(1)} %get-tuple-element.91), channel_id=1, source_target_pairs={{0,3},{1,2},{2,1},{3,0},{4,7},{5,6},{6,5},{7,4},{8,11},{9,10},{10,... | collective-permute-start | bytes 786440 | tf_op jit(solution)/shard_map/ppermute | solution.py:188
  57.2 23.3 %collective-permute-start.26 = (bf16[128,1024]{1,0:T(8,128)(2,1)S(1)}, bf16[128,1024]{1,0:T(8,128)(2,1)S(1)}, u32[]{:S(2)}, u32[]{:S(2)}) collective-permute-start(bf16[128,1024]{1,0:T(8,128)(2,1)S(1)} %get-tuple-element.93), channel_id=1, source_target_pairs={{0,1},{1,0},{2,3},{3,2},{4,5},{5,4},{6,7},{7,6},{8,9},{9,8},{10,11... | collective-permute-start | bytes 786440 | tf_op jit(solution)/shard_map/ppermute | solution.py:188

commit v2 on v1

--- a/solution.py
+++ b/solution.py
@@ -164,25 +164,15 @@
     return [(i, i ^ d) for i in range(size)]
 
 
-def relocate(partner, arrays):
-    nodes = lax.axis_size("node")
-    distance = lax.axis_index("node") ^ partner[lax.axis_index("node")]
-
-    def branch(d):
-        return lambda *held: tuple(lax.ppermute(a, "node", xor_pairs(nodes, d)) for a in held)
-
-    return lax.switch(distance - 1, [branch(d) for d in range(1, nodes)], *arrays)
-
-
-def on_device(tokens, grad_out, router_gate, counts, routes, partner, w_gate, w_up, w_down):
-    group = lax.axis_size("group")
+def pass_at(d, counts, routes, tokens, grad_out, gate, w_gate, w_up, w_down):
+    nodes, group = lax.axis_size("node"), lax.axis_size("group")
+    placed = [lax.ppermute(w, "node", xor_pairs(nodes, d)) if d else w for w in (w_gate, w_up, w_down)]
     order = sorted(range(1, group), key=lambda d: (d != 2, -d)) + [0]
     hops = [functools.partial(lambda d, me: me ^ d, d) for d in order]
-    packed = pack(hops, counts, routes, tokens, grad_out, router_gate)
+    packed = pack(hops, counts, routes, tokens, grad_out, gate)
     places = [
         lax.ppermute(place, "group", xor_pairs(group, d)) if d else place for d, place in zip(order, packed)
     ]
-    placed = relocate(partner, (w_gate[0], w_up[0], w_down[0]))
     results = [expert(place, *placed) for place in places]
     returned = [
         lax.ppermute(back, "group", xor_pairs(group, d)) if d else back for d, (back, _) in zip(order, results)
@@ -190,6 +180,24 @@
     grads = weights(places, [inner for _, inner in results])
     grad_tokens = combine(hops, counts, routes, returned)
     return (grad_tokens, *grads)
+
+
+def relocate(nodes, distance, arrays):
+    def branch(d):
+        return lambda *held: tuple(lax.ppermute(a, "node", xor_pairs(nodes, d)) for a in held)
+
+    return lax.switch(distance - 1, [branch(d) for d in range(1, nodes)], *arrays)
+
+
+def on_device(tokens, grad_out, router_gate, counts, routes, partner, w_gate, w_up, w_down):
+    nodes = lax.axis_size("node")
+    distance = lax.axis_index("node") ^ partner[lax.axis_index("node")]
+    rows = (counts, routes, tokens, grad_out, router_gate)
+    held = (w_gate[0], w_up[0], w_down[0])
+    if nodes > 8:
+        return pass_at(0, *rows, *relocate(nodes, distance, held))
+    branches = [functools.partial(pass_at, d) for d in range(1, nodes)]
+    return lax.switch(distance - 1, branches, *rows, *held)
 
 
 def solution(mesh):

time: 82.5 us -> 79.9 us (0.968)
  the two profiles are of different devices: /device:TPU:0 before, /device:TPU:21 now
where the time goes in v2:
time: 79.9 us; the launch traced here: 79.4 us
  waiting for transfers between devices  51.3 us (64%)
  starting transfers between devices  12.4 us (16%)
  Pallas kernels  11 us (14%)
  local copies, waits for them, and re-layouts  2.92 us (4%)
  between operations  1.33 us (2%)
    ppermute x3, waiting for transfers between devices, pass_at(): lax.ppermute(place, 'group', xor_pairs(group, d))  38.5 us
    ppermute x3, waiting for transfers between devices, pass_at(): lax.ppermute(back, 'group', xor_pairs(group, d))  12.8 us
    ppermute x3, starting transfers between devices, pass_at(): lax.ppermute(place, 'group', xor_pairs(group, d))  7.84 us
    pallas_call x4, Pallas kernels, expert(): pl.pallas_call(expert_kernel, out_shape=[jax.ShapeDtypeStruct((block, dep...  4.31 us
    ppermute x3, starting transfers between devices, pass_at(): lax.ppermute(back, 'group', xor_pairs(group, d))  2.95 us
    pallas_call x1, Pallas kernels, weights(): pl.pallas_call(functools.partial(weights_kernel, count), out_shape=[wide,...  2.9 us
    pallas_call x1, Pallas kernels, pack(): pl.pallas_call(functools.partial(pack_kernel, hops), out_shape=[place] *...  2.33 us
    unnamed x8, local copies, waits for them, and re-layouts  2.1 us
  transfers between devices with their start and end apart: 9, of which 4 were waited for; matrix products, arithmetic and copies ran while one was open for 0% of the time, Pallas kernels for 9%

profile of v2, /device:TPU:21, one launch (start us, length us, event | category | flops | bytes accessed | tf_op | source)
XLA Modules:
  0.0 79.4 jit_solution(4981658822445863973)
XLA Ops:
  0.6 0.0 copy-start.16
  0.6 0.6 copy-done.16
  1.3 0.6 dynamic_slice.3
  2.5 0.0 copy-start.1
  2.5 0.0 copy-start.17
  2.6 0.7 copy-done.1
  3.2 0.0 copy-done.17
  3.2 75.4 %conditional.1 = (bf16[1,1024,256]{2,1,0:T(8,128)(2,1)}, bf16[1,1024,256]{2,1,0:T(8,128)(2,1)}, bf16[1,256,1024]{2,1,0:T(8,128)(2,1)}, bf16[256,1024]{1,0:T(8,128)(2,1)S(1)}) conditional(s32[]{:T(128)} %clamp.3, (s32[1]{0:T(128)}, s32[1,2,1]{1,2,0:T(1,128)S(1)}, bf16[256,1024]{1,0:T(8,128)(2,1)}, ...), branch_computations={%region_0.0_spmd, %region_1.0_spmd, %region_2.0_spmd, %region_3.0_... | conditional | flops 2147483648 | bytes 30935504 | solution.py:200
  3.2 0.1 copy.26.routes
  3.3 0.1 copy.27.gate
  3.4 0.0 copy-start.5
  3.5 0.0 copy-start.12
  3.5 2.3 %pack.10 = (bf16[256,1024]{1,0:T(8,128)(2,1)S(1)}, bf16[256,1024]{1,0:T(8,128)(2,1)S(1)}, bf16[256,1024]{1,0:T(8,128)(2,1)S(1)}, bf16[256,1024]{1,0:T(8,128)(2,1)S(1)}) custom-call(s32[1]{0:T(128)} %get-tuple-element.181.counts, s32[1,2,1]{2,1,0:T(2,128)S(1)} %copy.26.routes, bf16[256,1024]{1,0:T(8,128)(2,1)} %get-tuple-element.183.tokens, ...), custom_call_target="tpu_custom_call" | custom-call | tf_op jit(solution)/shard_map/cond/branch_3_fun/pack/pallas_call | solution.py:48
  5.8 0.1 collective-permute-start.27
  5.9 0.0 copy-done.5
  5.9 0.2 collective-permute-start.28
  6.1 0.0 copy-done.12
  6.1 1.3 %collective-permute-start.29 = (bf16[1024,256]{1,0:T(8,128)(2,1)S(1)}, bf16[1024,256]{1,0:T(8,128)(2,1)S(1)}, u32[]{:S(2)}, u32[]{:S(2)}) collective-permute-start(bf16[1024,256]{1,0:T(8,128)(2,1)S(1)} %copy-done.12), channel_id=1, source_target_pairs={{0,16},{4,20},{8,24},{12,28},{16,0},{20,4},{24,8},{28,12},{1,17},{... | collective-permute-start | bytes 1572872 | tf_op jit(solution)/shard_map/cond/branch_3_fun/ppermute | solution.py:169
  7.4 0.1 collective-permute-start.30
  7.6 2.4 %collective-permute-start.32 = (bf16[256,1024]{1,0:T(8,128)(2,1)S(1)}, bf16[256,1024]{1,0:T(8,128)(2,1)S(1)}, u32[]{:S(2)}, u32[]{:S(2)}) collective-permute-start(bf16[256,1024]{1,0:T(8,128)(2,1)S(1)} %get-tuple-element.191), channel_id=1, source_target_pairs={{0,3},{1,2},{2,1},{3,0},{4,7},{5,6},{6,5},{7,4},{8,11},{9,10},{10,... | collective-permute-start | bytes 1572872 | tf_op jit(solution)/shard_map/cond/branch_3_fun/ppermute | solution.py:174
  9.9 28.9 %collective-permute-done.27.place.refs_0_ = bf16[256,1024]{1,0:T(8,128)(2,1)S(1)} collective-permute-done((bf16[256,1024]{1,0:T(8,128)(2,1)S(1)}, bf16[256,1024]{1,0:T(8,128)(2,1)S(1)}, u32[]{:S(2)}, u32[]{:S(2)}) %collective-permute-start.27) | collective-permute-done | bytes 524320 | tf_op jit(solution)/shard_map/cond/branch_3_fun/ppermute | solution.py:174
  38.9 5.4 %collective-permute-start.34 = (bf16[256,1024]{1,0:T(8,128)(2,1)S(1)}, bf16[256,1024]{1,0:T(8,128)(2,1)S(1)}, u32[]{:S(2)}, u32[]{:S(2)}) collective-permute-start(bf16[256,1024]{1,0:T(8,128)(2,1)S(1)} %get-tuple-element.193), channel_id=1, source_target_pairs={{0,1},{1,0},{2,3},{3,2},{4,5},{5,4},{6,7},{7,6},{8,9},{9,8},{10,11... | collective-permute-start | bytes 1572872 | tf_op jit(solution)/shard_map/cond/branch_3_fun/ppermute | solution.py:174
  44.3 0.0 collective-permute-done.28.w_gate
  44.3 0.0 collective-permute-done.29.w_up
  44.3 0.0 collective-permute-done.30.w_down
  44.3 1.1 %expert.40 = (bf16[128,1024]{1,0:T(8,128)(2,1)S(1)}, bf16[3,128,256]{2,1,0:T(8,128)(2,1)S(1)}) custom-call(bf16[256,1024]{1,0:T(8,128)(2,1)S(1)} %collective-permute-done.27.place.refs_0_, bf16[1024,256]{1,0:T(8,128)(2,1)S(1)} %collective-permute-done.28.w_gate, bf16[1024,256]{1,0:T(8,128)(2,1)S(1)} %collective-permute-done.29.w_up, ...), custom_call_target="tpu_custom_call" | custom-call | flops 335544320 | bytes 2097152 | tf_op jit(solution)/shard_map/cond/branch_3_fun/expert/pallas_call | solution.py:78
  45.4 0.1 collective-permute-start.31
  45.4 8.9 %collective-permute-done.32.place.refs_1_ = bf16[256,1024]{1,0:T(8,128)(2,1)S(1)} collective-permute-done((bf16[256,1024]{1,0:T(8,128)(2,1)S(1)}, bf16[256,1024]{1,0:T(8,128)(2,1)S(1)}, u32[]{:S(2)}, u32[]{:S(2)}) %collective-permute-start.32) | collective-permute-done | bytes 524320 | tf_op jit(solution)/shard_map/cond/branch_3_fun/ppermute | solution.py:174
  54.3 1.1 %expert.41 = (bf16[128,1024]{1,0:T(8,128)(2,1)S(1)}, bf16[3,128,256]{2,1,0:T(8,128)(2,1)S(1)}) custom-call(bf16[256,1024]{1,0:T(8,128)(2,1)S(1)} %collective-permute-done.32.place.refs_1_, bf16[1024,256]{1,0:T(8,128)(2,1)S(1)} %collective-permute-done.28.w_gate, bf16[1024,256]{1,0:T(8,128)(2,1)S(1)} %collective-permute-done.29.w_up, ...), custom_call_target="tpu_custom_call" | custom-call | flops 335544320 | bytes 2097152 | tf_op jit(solution)/shard_map/cond/branch_3_fun/expert/pallas_call | solution.py:78
  55.4 0.1 collective-permute-start.33
  55.5 0.6 collective-permute-done.34.place.refs_2_
  56.1 1.1 %expert.42 = (bf16[128,1024]{1,0:T(8,128)(2,1)S(1)}, bf16[3,128,256]{2,1,0:T(8,128)(2,1)S(1)}) custom-call(bf16[256,1024]{1,0:T(8,128)(2,1)S(1)} %collective-permute-done.34.place.refs_2_, bf16[1024,256]{1,0:T(8,128)(2,1)S(1)} %collective-permute-done.28.w_gate, bf16[1024,256]{1,0:T(8,128)(2,1)S(1)} %collective-permute-done.29.w_up, ...), custom_call_target="tpu_custom_call" | custom-call | flops 335544320 | bytes 2097152 | tf_op jit(solution)/shard_map/cond/branch_3_fun/expert/pallas_call | solution.py:78
  57.2 2.8 %collective-permute-start.35 = (bf16[128,1024]{1,0:T(8,128)(2,1)S(1)}, bf16[128,1024]{1,0:T(8,128)(2,1)S(1)}, u32[]{:S(2)}, u32[]{:S(2)}) collective-permute-start(bf16[128,1024]{1,0:T(8,128)(2,1)S(1)} %get-tuple-element.194), channel_id=1, source_target_pairs={{0,1},{1,0},{2,3},{3,2},{4,5},{5,4},{6,7},{7,6},{8,9},{9,8},{10,11... | collective-permute-start | bytes 786440 | tf_op jit(solution)/shard_map/cond/branch_3_fun/ppermute | solution.py:178
  60.0 1.1 %expert.43 = (bf16[128,1024]{1,0:T(8,128)(2,1)S(1)}, bf16[3,128,256]{2,1,0:T(8,128)(2,1)S(1)}) custom-call(bf16[256,1024]{1,0:T(8,128)(2,1)S(1)} %get-tuple-element.195.place.refs_3_, bf16[1024,256]{1,0:T(8,128)(2,1)S(1)} %collective-permute-done.28.w_gate, bf16[1024,256]{1,0:T(8,128)(2,1)S(1)} %collective-permute-done.29.w_up, ...), custom_call_target="tpu_custom_call" | custom-call | flops 335544320 | bytes 2097152 | tf_op jit(solution)/shard_map/cond/branch_3_fun/expert/pallas_call | solution.py:78
  61.1 2.9 %weight_grads.10 = (bf16[1,1024,256]{2,1,0:T(8,128)(2,1)}, bf16[1,1024,256]{2,1,0:T(8,128)(2,1)}, bf16[1,256,1024]{2,1,0:T(8,128)(2,1)}) custom-call(bf16[256,1024]{1,0:T(8,128)(2,1)S(1)} %collective-permute-done.27.place.refs_0_, bf16[256,1024]{1,0:T(8,128)(2,1)S(1)} %collective-permute-done.32.place.refs_1_, ...), custom_call_target="tpu_custom_call" | custom-call | flops 805306368 | bytes 2621440 | tf_op jit(solution)/shard_map/cond/branch_3_fun/weight_grads/pallas_call | solution.py:113
  64.0 0.0 collective-permute-done.31.refs_0_
  64.0 12.8 %collective-permute-done.33.refs_1_ = bf16[128,1024]{1,0:T(8,128)(2,1)S(1)} collective-permute-done((bf16[128,1024]{1,0:T(8,128)(2,1)S(1)}, bf16[128,1024]{1,0:T(8,128)(2,1)S(1)}, u32[]{:S(2)}, u32[]{:S(2)}) %collective-permute-start.33) | collective-permute-done | bytes 262176 | tf_op jit(solution)/shard_map/cond/branch_3_fun/ppermute | solution.py:178
  76.8 0.0 collective-permute-done.35.refs_2_
  76.8 1.4 %combine.10 = bf16[256,1024]{1,0:T(8,128)(2,1)S(1)} custom-call(s32[1]{0:T(128)} %get-tuple-element.181.counts, s32[1,2,1]{2,1,0:T(2,128)S(1)} %copy.26.routes, bf16[128,1024]{1,0:T(8,128)(2,1)S(1)} %collective-permute-done.31.refs_0_, bf16[128,1024]{1,0:T(8,128)(2,1)S(1)} %collective-permute-done.33.refs_1_, ...), custom_call_target="tpu_custom_call" | custom-call | tf_op jit(solution)/shard_map/cond/branch_3_fun/combine/pallas_call | solution.py:152
  78.6 0.0 copy-start
  78.6 0.8 copy-done
Async XLA Ops:
  0.6 0.7 copy-start.16
  2.5 0.7 copy-start.1
  2.5 0.7 copy-start.17
  3.4 2.4 %copy-start.5 = (bf16[1024,256]{1,0:T(8,128)(2,1)S(1)}, bf16[1024,256]{1,0:T(8,128)(2,1)}, u32[]{:S(2)}) copy-start(bf16[1024,256]{1,0:T(8,128)(2,1)} %get-tuple-element.187) | copy-start | bytes 1572868 | tf_op jit(solution)/shard_map/cond
  3.5 2.6 %copy-start.12 = (bf16[1024,256]{1,0:T(8,128)(2,1)S(1)}, bf16[1024,256]{1,0:T(8,128)(2,1)}, u32[]{:S(2)}) copy-start(bf16[1024,256]{1,0:T(8,128)(2,1)} %get-tuple-element.188) | copy-start | bytes 1572868 | tf_op jit(solution)/shard_map/cond
  5.8 33.1 %collective-permute-start.27 = (bf16[256,1024]{1,0:T(8,128)(2,1)S(1)}, bf16[256,1024]{1,0:T(8,128)(2,1)S(1)}, u32[]{:S(2)}, u32[]{:S(2)}) collective-permute-start(bf16[256,1024]{1,0:T(8,128)(2,1)S(1)} %get-tuple-element.186), channel_id=1, source_target_pairs={{0,2},{1,3},{2,0},{3,1},{4,6},{5,7},{6,4},{7,5},{8,10},{9,11},{10,... | collective-permute-start | bytes 1572872 | tf_op jit(solution)/shard_map/cond/branch_3_fun/ppermute | solution.py:174
  5.9 38.4 %collective-permute-start.28 = (bf16[1024,256]{1,0:T(8,128)(2,1)S(1)}, bf16[1024,256]{1,0:T(8,128)(2,1)S(1)}, u32[]{:S(2)}, u32[]{:S(2)}) collective-permute-start(bf16[1024,256]{1,0:T(8,128)(2,1)S(1)} %copy-done.5), channel_id=1, source_target_pairs={{0,16},{4,20},{8,24},{12,28},{16,0},{20,4},{24,8},{28,12},{1,17},{... | collective-permute-start | bytes 1572872 | tf_op jit(solution)/shard_map/cond/branch_3_fun/ppermute | solution.py:169
  6.1 38.2 %collective-permute-start.29 = (bf16[1024,256]{1,0:T(8,128)(2,1)S(1)}, bf16[1024,256]{1,0:T(8,128)(2,1)S(1)}, u32[]{:S(2)}, u32[]{:S(2)}) collective-permute-start(bf16[1024,256]{1,0:T(8,128)(2,1)S(1)} %copy-done.12), channel_id=1, source_target_pairs={{0,16},{4,20},{8,24},{12,28},{16,0},{20,4},{24,8},{28,12},{1,17},{... | collective-permute-start | bytes 1572872 | tf_op jit(solution)/shard_map/cond/branch_3_fun/ppermute | solution.py:169
  7.4 36.8 %collective-permute-start.30 = (bf16[256,1024]{1,0:T(8,128)(2,1)}, bf16[256,1024]{1,0:T(8,128)(2,1)S(1)}, u32[]{:S(2)}, u32[]{:S(2)}) collective-permute-start(bf16[256,1024]{1,0:T(8,128)(2,1)} %get-tuple-element.189), channel_id=1, source_target_pairs={{0,16},{4,20},{8,24},{12,28},{16,0},{20,4},{24,8},{28,12},{1,17},{... | collective-permute-start | bytes 1572872 | tf_op jit(solution)/shard_map/cond/branch_3_fun/ppermute | solution.py:169
  7.6 46.8 %collective-permute-start.32 = (bf16[256,1024]{1,0:T(8,128)(2,1)S(1)}, bf16[256,1024]{1,0:T(8,128)(2,1)S(1)}, u32[]{:S(2)}, u32[]{:S(2)}) collective-permute-start(bf16[256,1024]{1,0:T(8,128)(2,1)S(1)} %get-tuple-element.191), channel_id=1, source_target_pairs={{0,3},{1,2},{2,1},{3,0},{4,7},{5,6},{6,5},{7,4},{8,11},{9,10},{10,... | collective-permute-start | bytes 1572872 | tf_op jit(solution)/shard_map/cond/branch_3_fun/ppermute | solution.py:174
  38.9 17.2 %collective-permute-start.34 = (bf16[256,1024]{1,0:T(8,128)(2,1)S(1)}, bf16[256,1024]{1,0:T(8,128)(2,1)S(1)}, u32[]{:S(2)}, u32[]{:S(2)}) collective-permute-start(bf16[256,1024]{1,0:T(8,128)(2,1)S(1)} %get-tuple-element.193), channel_id=1, source_target_pairs={{0,1},{1,0},{2,3},{3,2},{4,5},{5,4},{6,7},{7,6},{8,9},{9,8},{10,11... | collective-permute-start | bytes 1572872 | tf_op jit(solution)/shard_map/cond/branch_3_fun/ppermute | solution.py:174
  45.4 18.6 %collective-permute-start.31 = (bf16[128,1024]{1,0:T(8,128)(2,1)S(1)}, bf16[128,1024]{1,0:T(8,128)(2,1)S(1)}, u32[]{:S(2)}, u32[]{:S(2)}) collective-permute-start(bf16[128,1024]{1,0:T(8,128)(2,1)S(1)} %get-tuple-element.190), channel_id=1, source_target_pairs={{0,2},{1,3},{2,0},{3,1},{4,6},{5,7},{6,4},{7,5},{8,10},{9,11},{10,... | collective-permute-start | bytes 786440 | tf_op jit(solution)/shard_map/cond/branch_3_fun/ppermute | solution.py:178
  55.4 21.4 %collective-permute-start.33 = (bf16[128,1024]{1,0:T(8,128)(2,1)S(1)}, bf16[128,1024]{1,0:T(8,128)(2,1)S(1)}, u32[]{:S(2)}, u32[]{:S(2)}) collective-permute-start(bf16[128,1024]{1,0:T(8,128)(2,1)S(1)} %get-tuple-element.192), channel_id=1, source_target_pairs={{0,3},{1,2},{2,1},{3,0},{4,7},{5,6},{6,5},{7,4},{8,11},{9,10},{10,... | collective-permute-start | bytes 786440 | tf_op jit(solution)/shard_map/cond/branch_3_fun/ppermute | solution.py:178
  57.2 19.6 %collective-permute-start.35 = (bf16[128,1024]{1,0:T(8,128)(2,1)S(1)}, bf16[128,1024]{1,0:T(8,128)(2,1)S(1)}, u32[]{:S(2)}, u32[]{:S(2)}) collective-permute-start(bf16[128,1024]{1,0:T(8,128)(2,1)S(1)} %get-tuple-element.194), channel_id=1, source_target_pairs={{0,1},{1,0},{2,3},{3,2},{4,5},{5,4},{6,7},{7,6},{8,9},{9,8},{10,11... | collective-permute-start | bytes 786440 | tf_op jit(solution)/shard_map/cond/branch_3_fun/ppermute | solution.py:178
  78.6 0.8 %copy-start = (bf16[256,1024]{1,0:T(8,128)(2,1)}, bf16[256,1024]{1,0:T(8,128)(2,1)S(1)}, u32[]{:S(2)}) copy-start(bf16[256,1024]{1,0:T(8,128)(2,1)S(1)} %get-tuple-element.277) | copy-start | bytes 1572868

commit v3 on v1

v3 whole, which is shorter than its diff:
```python
import functools

import jax
import jax.numpy as jnp
from jax import lax
from jax.experimental import pallas as pl
from jax.experimental.pallas import tpu as pltpu
from jax.sharding import PartitionSpec as P

VMEM = pltpu.VMEM
SMEM = pltpu.SMEM
LIMIT = 48 * 1024 * 1024


def dot(left, right, dims):
    return lax.dot_general(left, right, (dims, ((), ())), preferred_element_type=jnp.float32)


def params():
    return pltpu.CompilerParams(vmem_limit_bytes=LIMIT)


def in_hbm(array):
    return pltpu.with_memory_space_constraint(array, pltpu.HBM)


def spec(space):
    return pl.BlockSpec(memory_space=space)


def pack_kernel(hops, shape, counts, partner, routes, tokens, grad_out, gate, w_gate, w_up, w_down, *refs):
    slots, topk = shape
    places, (stack, plan, goals) = refs[: len(hops)], refs[len(hops) : len(hops) + 3]
    partner_s, routes_s, grads_v, gate_v, sems, place_sems, stack_sems = refs[len(hops) + 3 :]
    depth, width = w_gate.shape[1:]
    squares = depth // width
    first = [
        pltpu.make_async_copy(routes, routes_s, sems.at[0]),
        pltpu.make_async_copy(partner, partner_s, sems.at[1]),
        pltpu.make_async_copy(gate, gate_v, sems.at[2]),
        pltpu.make_async_copy(grad_out, grads_v, sems.at[3]),
    ]
    stacked = [
        pltpu.make_async_copy(w_gate.at[0], stack.at[pl.ds(0, depth)], stack_sems.at[0]),
        pltpu.make_async_copy(w_up.at[0], stack.at[pl.ds(depth, depth)], stack_sems.at[1]),
    ] + [
        pltpu.make_async_copy(
            w_down.at[0, :, pl.ds(i * width, width)],
            stack.at[pl.ds(2 * depth + i * width, width)],
            stack_sems.at[2 + i],
        )
        for i in range(squares)
    ]
    for copy in first + stacked:
        copy.start()
    block = grads_v.shape[0] // slots
    me, node = lax.axis_index("group"), lax.axis_index("node")
    first[0].wait()
    entries = [(b, k) for b in range(slots) for k in range(topk)]
    sent = [[(routes_s[b * topk + k] == hop(me)) & (b < counts[0]) for b, k in entries] for hop in hops]

    def tokens_to(place, b, i):
        return pltpu.make_async_copy(tokens.at[pl.ds(b * block, block)], place.at[pl.ds(0, block)], place_sems.at[i])

    for i, place in enumerate(places):
        for (b, k), found in zip(entries, sent[i]):

            @pl.when(found)
            def _():
                tokens_to(place, b, i).start()

    for i, place in enumerate(places):

        @pl.when(jnp.logical_not(functools.reduce(jnp.logical_or, sent[i])))
        def _():
            place[...] = jnp.zeros_like(place)

    for copy in first[1:]:
        copy.wait()
    plan[0] = (node ^ partner_s[node]) - 1
    for i, (b, _) in enumerate(entries):
        goals[i] = jnp.where(b < counts[0], routes_s[i], -1)
    for i, place in enumerate(places):
        for (b, k), found in zip(entries, sent[i]):

            @pl.when(found)
            def _():
                rows = pl.ds(b * block, block)
                scaled = gate_v[k : k + 1, rows].T * grads_v[rows].astype(jnp.float32)
                place[block:] = scaled.astype(jnp.bfloat16)

    for i, place in enumerate(places):
        for (b, k), found in zip(entries, sent[i]):

            @pl.when(found)
            def _():
                tokens_to(place, b, i).wait()

    for copy in stacked:
        copy.wait()


def pack(hops, partner, counts, routes, tokens, grad_out, gate, w_gate, w_up, w_down):
    slots, topk = routes.shape[1], routes.shape[2]
    length, depth = tokens.shape
    width = w_gate.shape[2]
    place = jax.ShapeDtypeStruct((2 * length // slots, depth), jnp.bfloat16)
    *places, stack, plan, goals = pl.pallas_call(
        functools.partial(pack_kernel, hops, (slots, topk)),
        out_shape=[place] * len(hops)
        + [jax.ShapeDtypeStruct((3 * depth, width), jnp.bfloat16)]
        + [SMEM((1,), jnp.int32), SMEM((slots * topk,), jnp.int32)],
        in_specs=[spec(SMEM)] + [spec(pltpu.HBM)] * 8,
        out_specs=[spec(VMEM)] * (len(hops) + 1) + [spec(SMEM)] * 2,
        scratch_shapes=[
            SMEM(partner.shape, jnp.int32),
            SMEM((slots * topk,), jnp.int32),
            VMEM((length, depth), jnp.bfloat16),
            VMEM((topk, length), jnp.float32),
            pltpu.SemaphoreType.DMA((4,)),
            pltpu.SemaphoreType.DMA((len(hops),)),
            pltpu.SemaphoreType.DMA((2 + depth // width,)),
        ],
        compiler_params=params(),
        name="pack",
    )(counts, *map(in_hbm, (partner, routes.reshape(slots * topk), tokens, grad_out, gate.T, w_gate, w_up, w_down)))
    return places, stack, plan, goals


def expert_kernel(place, stack, back, inner):
    block, depth = place.shape[0] // 2, place.shape[1]
    width = stack.shape[1]
    rows, grads = place[:block], place[block:]
    gate_w, up_w = stack[:depth], stack[depth : 2 * depth]
    gate_pre = dot(rows, gate_w, ((1,), (0,)))
    up_pre = dot(rows, up_w, ((1,), (0,)))
    sig = 1.0 / (1.0 + jnp.exp(-gate_pre))
    swish = gate_pre * sig
    grad_hidden = jnp.zeros_like(gate_pre)
    for i in range(0, depth, width):
        square = stack[2 * depth + i : 2 * depth + i + width]
        grad_hidden += dot(grads[:, i : i + width], square, ((1,), (1,)))
    grad_upre = (grad_hidden * swish).astype(jnp.bfloat16)
    grad_gpre = (grad_hidden * up_pre * sig * (1.0 + gate_pre * (1.0 - sig))).astype(jnp.bfloat16)
    back[...] = (dot(grad_gpre, gate_w, ((1,), (1,))) + dot(grad_upre, up_w, ((1,), (1,)))).astype(jnp.bfloat16)
    inner[0] = grad_gpre
    inner[1] = grad_upre
    inner[2] = (swish * up_pre).astype(jnp.bfloat16)


def expert(place, stack):
    block, depth = place.shape[0] // 2, place.shape[1]
    width = stack.shape[1]
    return pl.pallas_call(
        expert_kernel,
        out_shape=[
            jax.ShapeDtypeStruct((block, depth), jnp.bfloat16),
            jax.ShapeDtypeStruct((3, block, width), jnp.bfloat16),
        ],
        in_specs=[spec(VMEM)] * 2,
        out_specs=[spec(VMEM)] * 2,
        compiler_params=params(),
        cost_estimate=pl.CostEstimate(
            flops=10 * block * depth * width, bytes_accessed=8 * depth * width, transcendentals=block * width
        ),
        name="expert",
    )(place, stack)


def weights_kernel(count, *refs):
    places, inners = refs[:count], refs[count : 2 * count]
    grad_gate, grad_up, grad_down = refs[2 * count :]
    block = places[0].shape[0] // 2
    rows = jnp.concatenate([place[:block] for place in places], axis=0)
    grads = jnp.concatenate([place[block:] for place in places], axis=0)
    gpre, upre, hidden = (jnp.concatenate([inner[i] for inner in inners], axis=0) for i in range(3))
    grad_gate[0] = dot(rows, gpre, ((0,), (0,))).astype(jnp.bfloat16)
    grad_up[0] = dot(rows, upre, ((0,), (0,))).astype(jnp.bfloat16)
    grad_down[0] = dot(hidden, grads, ((0,), (0,))).astype(jnp.bfloat16)


def weights(places, inners):
    count = len(places)
    block, depth = places[0].shape[0] // 2, places[0].shape[1]
    width = inners[0].shape[2]
    tile = min(depth, 256)
    wide = jax.ShapeDtypeStruct((1, depth, width), jnp.bfloat16)
    tall = jax.ShapeDtypeStruct((1, width, depth), jnp.bfloat16)
    return pl.pallas_call(
        functools.partial(weights_kernel, count),
        out_shape=[wide, wide, tall],
        grid=(depth // tile,),
        in_specs=[pl.BlockSpec((2 * block, tile), lambda i: (0, i))] * count
        + [pl.BlockSpec((3, block, width), lambda i: (0, 0, 0))] * count,
        out_specs=[
            pl.BlockSpec((1, tile, width), lambda i: (0, i, 0)),
            pl.BlockSpec((1, tile, width), lambda i: (0, i, 0)),
            pl.BlockSpec((1, width, tile), lambda i: (0, 0, i)),
        ],
        compiler_params=params(),
        cost_estimate=pl.CostEstimate(
            flops=6 * count * block * depth * width, bytes_accessed=10 * depth * width, transcendentals=0
        ),
        name="weight_grads",
    )(*places, *inners)


def settle_kernel(hops, shape, goals, *refs):
    returned, out, empty, sems = refs[: len(hops)], refs[len(hops)], refs[len(hops) + 1], refs[len(hops) + 2]
    slots = shape[0]
    block = empty.shape[0]
    me = lax.axis_index("group")
    empty[...] = jnp.zeros_like(empty)
    for b in range(slots):
        target = out.at[pl.ds(b * block, block)]
        for hop, part in zip(hops, returned):

            @pl.when(goals[b] == hop(me))
            def _():
                pltpu.make_async_copy(part, target, sems.at[b]).start()

        @pl.when(goals[b] < 0)
        def _():
            pltpu.make_async_copy(empty, target, sems.at[b]).start()

    for b in range(slots):
        pltpu.make_async_copy(empty, out.at[pl.ds(b * block, block)], sems.at[b]).wait()


def combine_kernel(hops, shape, goals, *refs):
    returned, out, total = refs[: len(hops)], refs[len(hops)], refs[len(hops) + 1]
    slots, topk = shape
    block = out.shape[0] // slots
    me = lax.axis_index("group")
    for b in range(slots):
        total[...] = jnp.zeros_like(total)
        for k in range(topk):
            for hop, part in zip(hops, returned):

                @pl.when(goals[b * topk + k] == hop(me))
                def _():
                    total[...] += part[...].astype(jnp.float32)

        out[b * block : (b + 1) * block] = total[...].astype(jnp.bfloat16)


def combine(hops, shape, goals, returned):
    slots, topk = shape
    block, depth = returned[0].shape
    if topk == 1:
        kernel, where_from, where_to = settle_kernel, pl.ANY, pltpu.HBM
        scratch = [VMEM((block, depth), jnp.bfloat16), pltpu.SemaphoreType.DMA((slots,))]
    else:
        kernel, where_from, where_to = combine_kernel, VMEM, VMEM
        scratch = [VMEM((block, depth), jnp.float32)]
    return pl.pallas_call(
        functools.partial(kernel, hops, (slots, topk)),
        out_shape=where_to((slots * block, depth), jnp.bfloat16),
        in_specs=[spec(SMEM)] + [spec(where_from)] * len(hops),
        out_specs=spec(where_to),
        scratch_shapes=scratch,
        compiler_params=params(),
        name="combine",
    )(goals, *returned)


def xor_pairs(size, d):
    return [(i, i ^ d) for i in range(size)]


def pass_at(d, order, hops, shape, goals, stack, *packed):
    nodes, group = lax.axis_size("node"), lax.axis_size("group")
    stack = lax.ppermute(stack, "node", xor_pairs(nodes, d)) if d else stack
    places = [
        lax.ppermute(place, "group", xor_pairs(group, d)) if d else place for d, place in zip(order, packed)
    ]
    results = []
    for place in places:
        results.append(expert(place, stack))
        stack, _ = lax.optimization_barrier((stack, results[-1][1]))
    returned = [
        lax.ppermute(back, "group", xor_pairs(group, d)) if d else back for d, (back, _) in zip(order, results)
    ]
    grads = weights(places, [inner for _, inner in results])
    grad_tokens = combine(hops, shape, goals, returned)
    return (grad_tokens, *grads)


def on_device(tokens, grad_out, router_gate, counts, routes, partner, w_gate, w_up, w_down):
    nodes, group = lax.axis_size("node"), lax.axis_size("group")
    shape = routes.shape[1:]
    order = sorted(range(1, group), key=lambda d: (d != 2, -d)) + [0]
    hops = [functools.partial(lambda d, me: me ^ d, d) for d in order]
    packed, stack, plan, goals = pack(hops, partner, counts, routes, tokens, grad_out, router_gate, w_gate, w_up, w_down)
    if nodes > 8:
        moves = [
            functools.partial(lax.ppermute, axis_name="node", perm=xor_pairs(nodes, d)) for d in range(1, nodes)
        ]
        return pass_at(0, order, hops, shape, goals, lax.switch(plan[0], moves, stack), *packed)
    branches = [functools.partial(pass_at, d, order, hops, shape) for d in range(1, nodes)]
    return lax.switch(plan[0], branches, goals, stack, *packed)


def solution(mesh):
    both = ("node", "group")
    rows = P(both, None)
    cube = P(both, None, None)
    return jax.shard_map(
        on_device,
        mesh=mesh,
        in_specs=(rows, rows, rows, P(both), cube, P(), cube, cube, cube),
        out_specs=(rows, cube, cube, cube),
        check_vma=False,
    )
```

time: 82.5 us -> 79.1 us (0.959)
  Pallas kernels: 15.1 us -> 10.2 us
  local copies, waits for them, and re-layouts: 4.13 us -> 0 us
  waiting for transfers between devices: 32.8 us -> 36 us
  starting transfers between devices: 28 us -> 30.2 us
    pallas_call x4, Pallas kernels: 9.78 us -> 4.33 us  [expert(): pl.pallas_call(expert_kernel, out_shape=[jax.ShapeDtypeStruct((block, dep...]
    unnamed x12 -> x0, local copies, waits for them, and re-layouts: 3.54 us -> none
    ppermute x9 -> x7, waiting for transfers between devices: 32.8 us -> 36 us  [the longest x3 33.8 us: pass_at(): lax.ppermute(place, 'group', xor_pairs(group, d))]
    ppermute x9 -> x7, starting transfers between devices: 28 us -> 30.2 us  [the longest x3 24.5 us: pass_at(): lax.ppermute(back, 'group', xor_pairs(group, d))]
  transfers between devices with their start and end apart: 9 -> 7, of which waited for: 6 -> 2; matrix products, arithmetic and copies ran while one was open for 1% -> 0% of each run, Pallas kernels for 15% -> 9%
where the time goes in v3:
time: 79.1 us; the launch traced here: 78.2 us
  waiting for transfers between devices  36 us (46%)
  starting transfers between devices  30.2 us (38%)
  Pallas kernels  10.2 us (13%)
  between operations  1.49 us (2%)
    ppermute x3, waiting for transfers between devices, pass_at(): lax.ppermute(place, 'group', xor_pairs(group, d))  33.8 us
    ppermute x3, starting transfers between devices, pass_at(): lax.ppermute(back, 'group', xor_pairs(group, d))  24.5 us
    ppermute x3, starting transfers between devices, pass_at(): lax.ppermute(place, 'group', xor_pairs(group, d))  5.24 us
    pallas_call x4, Pallas kernels, expert(): pl.pallas_call(expert_kernel, out_shape=[jax.ShapeDtypeStruct((block, dep...  4.33 us
    pallas_call x1, Pallas kernels, weights(): pl.pallas_call(functools.partial(weights_kernel, count), out_shape=[wide,...  2.9 us
    ppermute x3, waiting for transfers between devices, pass_at(): lax.ppermute(back, 'group', xor_pairs(group, d))  2.22 us
    pallas_call x1, Pallas kernels, pack(): pl.pallas_call(functools.partial(pack_kernel, hops, (slots, topk)), out_s...  2.13 us
  transfers between devices with their start and end apart: 7, of which 2 were waited for; matrix products, arithmetic and copies ran while one was open for 0% of the time, Pallas kernels for 9%

profile of v3, /device:TPU:0, one launch (start us, length us, event | category | flops | bytes accessed | tf_op | source)
XLA Modules:
  0.0 78.2 jit_solution(5568350093235512353)
XLA Ops:
  1.3 2.1 %pack.1 = (bf16[256,1024]{1,0:T(8,128)(2,1)S(1)}, bf16[256,1024]{1,0:T(8,128)(2,1)S(1)}, bf16[256,1024]{1,0:T(8,128)(2,1)S(1)}, bf16[256,1024]{1,0:T(8,128)(2,1)...) custom-call(s32[1]{0:T(128)S(6)} %copy.48.counts, s32[8]{0:T(128)} %partner.1, s32[2]{0:T(128)} %bitcast.4, ...), custom_call_target="tpu_custom_call" | custom-call | tf_op jit(solution)/shard_map/pack/pallas_call | solution.py:108
  3.4 74.6 %conditional.1 = (bf16[1,1024,256]{2,1,0:T(8,128)(2,1)}, bf16[1,1024,256]{2,1,0:T(8,128)(2,1)}, bf16[1,256,1024]{2,1,0:T(8,128)(2,1)}, bf16[256,1024]{1,0:T(8,128)(2,1)}) conditional(s32[]{:T(128)} %bitcast.2, (bf16[256,1024]{1,0:T(8,128)(2,1)S(1)}, bf16[3072,256]{1,0:T(8,128)(2,1)S(1)}, ...), branch_computations={%region_0.0_spmd, %region_1.0_spmd, %region_2.0_spmd, %region_3.0_... | conditional | flops 2147483648 | bytes 26739000 | solution.py:301
  3.4 0.4 collective-permute-start.1
  3.9 3.7 %collective-permute-start = (bf16[256,1024]{1,0:T(8,128)(2,1)S(1)}, bf16[256,1024]{1,0:T(8,128)(2,1)S(1)}, u32[]{:S(2)}, u32[]{:S(2)}) collective-permute-start(bf16[256,1024]{1,0:T(8,128)(2,1)S(1)} %get-tuple-element.85), channel_id=1, source_target_pairs={{0,2},{1,3},{2,0},{3,1},{4,6},{5,7},{6,4},{7,5},{8,10},{9,11},{10,... | collective-permute-start | bytes 1572872 | tf_op jit(solution)/shard_map/cond/branch_0_fun/ppermute | solution.py:275
  7.6 1.3 %collective-permute-start.3 = (bf16[256,1024]{1,0:T(8,128)(2,1)S(1)}, bf16[256,1024]{1,0:T(8,128)(2,1)S(1)}, u32[]{:S(2)}, u32[]{:S(2)}) collective-permute-start(bf16[256,1024]{1,0:T(8,128)(2,1)S(1)} %get-tuple-element.88), channel_id=1, source_target_pairs={{0,3},{1,2},{2,1},{3,0},{4,7},{5,6},{6,5},{7,4},{8,11},{9,10},{10,... | collective-permute-start | bytes 1572872 | tf_op jit(solution)/shard_map/cond/branch_0_fun/ppermute | solution.py:275
  9.0 0.2 collective-permute-start.5
  9.1 33.8 %collective-permute-done.place.refs_0_ = bf16[256,1024]{1,0:T(8,128)(2,1)S(1)} collective-permute-done((bf16[256,1024]{1,0:T(8,128)(2,1)S(1)}, bf16[256,1024]{1,0:T(8,128)(2,1)S(1)}, u32[]{:S(2)}, u32[]{:S(2)}) %collective-permute-start) | collective-permute-done | bytes 524320 | tf_op jit(solution)/shard_map/cond/branch_0_fun/ppermute | solution.py:275
  42.9 0.0 collective-permute-done.1.stack
  42.9 1.1 %expert.28 = (bf16[128,1024]{1,0:T(8,128)(2,1)S(1)}, bf16[3,128,256]{2,1,0:T(8,128)(2,1)S(1)}) custom-call(bf16[256,1024]{1,0:T(8,128)(2,1)S(1)} %collective-permute-done.place.refs_0_, bf16[3072,256]{1,0:T(8,128)(2,1)S(1)} %collective-permute-done.1.stack), custom_call_target="tpu_custom_call" | custom-call | flops 335544320 | bytes 2097152 | tf_op jit(solution)/shard_map/cond/branch_0_fun/expert/pallas_call | solution.py:154
  44.0 0.1 collective-permute-start.2
  44.1 0.0 collective-permute-done.3.place.refs_1_
  44.1 1.1 %expert.29 = (bf16[128,1024]{1,0:T(8,128)(2,1)S(1)}, bf16[3,128,256]{2,1,0:T(8,128)(2,1)S(1)}) custom-call(bf16[256,1024]{1,0:T(8,128)(2,1)S(1)} %collective-permute-done.3.place.refs_1_, bf16[3072,256]{1,0:T(8,128)(2,1)S(1)} %collective-permute-done.1.stack), custom_call_target="tpu_custom_call" | custom-call | flops 335544320 | bytes 2097152 | tf_op jit(solution)/shard_map/cond/branch_0_fun/expert/pallas_call | solution.py:154
  45.2 3.4 %collective-permute-start.4 = (bf16[128,1024]{1,0:T(8,128)(2,1)S(1)}, bf16[128,1024]{1,0:T(8,128)(2,1)S(1)}, u32[]{:S(2)}, u32[]{:S(2)}) collective-permute-start(bf16[128,1024]{1,0:T(8,128)(2,1)S(1)} %get-tuple-element.91), channel_id=1, source_target_pairs={{0,3},{1,2},{2,1},{3,0},{4,7},{5,6},{6,5},{7,4},{8,11},{9,10},{10,... | collective-permute-start | bytes 786440 | tf_op jit(solution)/shard_map/cond/branch_0_fun/ppermute | solution.py:282
  48.6 0.0 collective-permute-done.5.place.refs_2_
  48.6 1.1 %expert.30 = (bf16[128,1024]{1,0:T(8,128)(2,1)S(1)}, bf16[3,128,256]{2,1,0:T(8,128)(2,1)S(1)}) custom-call(bf16[256,1024]{1,0:T(8,128)(2,1)S(1)} %collective-permute-done.5.place.refs_2_, bf16[3072,256]{1,0:T(8,128)(2,1)S(1)} %collective-permute-done.1.stack), custom_call_target="tpu_custom_call" | custom-call | flops 335544320 | bytes 2097152 | tf_op jit(solution)/shard_map/cond/branch_0_fun/expert/pallas_call | solution.py:154
  49.7 21.0 %collective-permute-start.6 = (bf16[128,1024]{1,0:T(8,128)(2,1)S(1)}, bf16[128,1024]{1,0:T(8,128)(2,1)S(1)}, u32[]{:S(2)}, u32[]{:S(2)}) collective-permute-start(bf16[128,1024]{1,0:T(8,128)(2,1)S(1)} %get-tuple-element.95), channel_id=1, source_target_pairs={{0,1},{1,0},{2,3},{3,2},{4,5},{5,4},{6,7},{7,6},{8,9},{9,8},{10,11... | collective-permute-start | bytes 786440 | tf_op jit(solution)/shard_map/cond/branch_0_fun/ppermute | solution.py:282
  70.7 1.1 %expert.31 = (bf16[128,1024]{1,0:T(8,128)(2,1)S(1)}, bf16[3,128,256]{2,1,0:T(8,128)(2,1)S(1)}) custom-call(bf16[256,1024]{1,0:T(8,128)(2,1)S(1)} %get-tuple-element.96.place.refs_3_, bf16[3072,256]{1,0:T(8,128)(2,1)S(1)} %collective-permute-done.1.stack), custom_call_target="tpu_custom_call" | custom-call | flops 335544320 | bytes 2097152 | tf_op jit(solution)/shard_map/cond/branch_0_fun/expert/pallas_call | solution.py:154
  71.8 2.9 %weight_grads.7 = (bf16[1,1024,256]{2,1,0:T(8,128)(2,1)}, bf16[1,1024,256]{2,1,0:T(8,128)(2,1)}, bf16[1,256,1024]{2,1,0:T(8,128)(2,1)}) custom-call(bf16[256,1024]{1,0:T(8,128)(2,1)S(1)} %collective-permute-done.place.refs_0_, bf16[256,1024]{1,0:T(8,128)(2,1)S(1)} %collective-permute-done.3.place.refs_1_, ...), custom_call_target="tpu_custom_call" | custom-call | flops 805306368 | bytes 2621440 | tf_op jit(solution)/shard_map/cond/branch_0_fun/weight_grads/pallas_call | solution.py:189
  74.7 0.0 collective-permute-done.2.refs_0_
  74.7 0.0 collective-permute-done.4.refs_1_
  74.7 2.2 %collective-permute-done.6.refs_2_ = bf16[128,1024]{1,0:T(8,128)(2,1)S(1)} collective-permute-done((bf16[128,1024]{1,0:T(8,128)(2,1)S(1)}, bf16[128,1024]{1,0:T(8,128)(2,1)S(1)}, u32[]{:S(2)}, u32[]{:S(2)}) %collective-permute-start.6) | collective-permute-done | bytes 262176 | tf_op jit(solution)/shard_map/cond/branch_0_fun/ppermute | solution.py:282
  76.9 0.8 %combine.7 = bf16[256,1024]{1,0:T(8,128)(2,1)} custom-call(s32[2]{0:T(128)S(4)} %get-tuple-element.84.goals, bf16[128,1024]{1,0:T(8,128)(2,1)S(1)} %collective-permute-done.2.refs_0_, bf16[128,1024]{1,0:T(8,128)(2,1)S(1)} %collective-permute-done.4.refs_1_, bf16[128,1024]{1,0:T(8,128)(2,1)S(1)} %collective-permute-done.6.refs_2_, ...), custom_call_target="tpu_custom_call" | custom-call | tf_op jit(solution)/shard_map/cond/branch_0_fun/combine/pallas_call | solution.py:256
Async XLA Ops:
  3.4 39.5 %collective-permute-start.1 = (bf16[3072,256]{1,0:T(8,128)(2,1)S(1)}, bf16[3072,256]{1,0:T(8,128)(2,1)S(1)}, u32[]{:S(2)}, u32[]{:S(2)}) collective-permute-start(bf16[3072,256]{1,0:T(8,128)(2,1)S(1)} %get-tuple-element.86), channel_id=1, source_target_pairs={{0,4},{4,0},{8,12},{12,8},{16,20},{20,16},{24,28},{28,24},{1,5},{5... | collective-permute-start | bytes 4718600 | tf_op jit(solution)/shard_map/cond/branch_0_fun/ppermute | solution.py:273
  3.9 39.0 %collective-permute-start = (bf16[256,1024]{1,0:T(8,128)(2,1)S(1)}, bf16[256,1024]{1,0:T(8,128)(2,1)S(1)}, u32[]{:S(2)}, u32[]{:S(2)}) collective-permute-start(bf16[256,1024]{1,0:T(8,128)(2,1)S(1)} %get-tuple-element.85), channel_id=1, source_target_pairs={{0,2},{1,3},{2,0},{3,1},{4,6},{5,7},{6,4},{7,5},{8,10},{9,11},{10,... | collective-permute-start | bytes 1572872 | tf_op jit(solution)/shard_map/cond/branch_0_fun/ppermute | solution.py:275
  7.6 36.5 %collective-permute-start.3 = (bf16[256,1024]{1,0:T(8,128)(2,1)S(1)}, bf16[256,1024]{1,0:T(8,128)(2,1)S(1)}, u32[]{:S(2)}, u32[]{:S(2)}) collective-permute-start(bf16[256,1024]{1,0:T(8,128)(2,1)S(1)} %get-tuple-element.88), channel_id=1, source_target_pairs={{0,3},{1,2},{2,1},{3,0},{4,7},{5,6},{6,5},{7,4},{8,11},{9,10},{10,... | collective-permute-start | bytes 1572872 | tf_op jit(solution)/shard_map/cond/branch_0_fun/ppermute | solution.py:275
  9.0 39.6 %collective-permute-start.5 = (bf16[256,1024]{1,0:T(8,128)(2,1)S(1)}, bf16[256,1024]{1,0:T(8,128)(2,1)S(1)}, u32[]{:S(2)}, u32[]{:S(2)}) collective-permute-start(bf16[256,1024]{1,0:T(8,128)(2,1)S(1)} %get-tuple-element.92), channel_id=1, source_target_pairs={{0,1},{1,0},{2,3},{3,2},{4,5},{5,4},{6,7},{7,6},{8,9},{9,8},{10,11... | collective-permute-start | bytes 1572872 | tf_op jit(solution)/shard_map/cond/branch_0_fun/ppermute | solution.py:275
  44.0 30.7 %collective-permute-start.2 = (bf16[128,1024]{1,0:T(8,128)(2,1)S(1)}, bf16[128,1024]{1,0:T(8,128)(2,1)S(1)}, u32[]{:S(2)}, u32[]{:S(2)}) collective-permute-start(bf16[128,1024]{1,0:T(8,128)(2,1)S(1)} %get-tuple-element.87), channel_id=1, source_target_pairs={{0,2},{1,3},{2,0},{3,1},{4,6},{5,7},{6,4},{7,5},{8,10},{9,11},{10,... | collective-permute-start | bytes 786440 | tf_op jit(solution)/shard_map/cond/branch_0_fun/ppermute | solution.py:282
  45.2 29.5 %collective-permute-start.4 = (bf16[128,1024]{1,0:T(8,128)(2,1)S(1)}, bf16[128,1024]{1,0:T(8,128)(2,1)S(1)}, u32[]{:S(2)}, u32[]{:S(2)}) collective-permute-start(bf16[128,1024]{1,0:T(8,128)(2,1)S(1)} %get-tuple-element.91), channel_id=1, source_target_pairs={{0,3},{1,2},{2,1},{3,0},{4,7},{5,6},{6,5},{7,4},{8,11},{9,10},{10,... | collective-permute-start | bytes 786440 | tf_op jit(solution)/shard_map/cond/branch_0_fun/ppermute | solution.py:282
  49.7 27.2 %collective-permute-start.6 = (bf16[128,1024]{1,0:T(8,128)(2,1)S(1)}, bf16[128,1024]{1,0:T(8,128)(2,1)S(1)}, u32[]{:S(2)}, u32[]{:S(2)}) collective-permute-start(bf16[128,1024]{1,0:T(8,128)(2,1)S(1)} %get-tuple-element.95), channel_id=1, source_target_pairs={{0,1},{1,0},{2,3},{3,2},{4,5},{5,4},{6,7},{7,6},{8,9},{9,8},{10,11... | collective-permute-start | bytes 786440 | tf_op jit(solution)/shard_map/cond/branch_0_fun/ppermute | solution.py:282

commit v4 on v3

--- a/solution.py
+++ b/solution.py
@@ -26,6 +26,9 @@
 
 def spec(space):
     return pl.BlockSpec(memory_space=space)
+
+
+EMPTY = 64.0
 
 
 def pack_kernel(hops, shape, counts, partner, routes, tokens, grad_out, gate, w_gate, w_up, w_down, *refs):
@@ -73,7 +76,7 @@
 
         @pl.when(jnp.logical_not(functools.reduce(jnp.logical_or, sent[i])))
         def _():
-            place[...] = jnp.zeros_like(place)
+            place[...] = jnp.full(place.shape, EMPTY, place.dtype)
 
     for copy in first[1:]:
         copy.wait()
@@ -127,7 +130,7 @@
     return places, stack, plan, goals
 
 
-def expert_kernel(place, stack, back, inner):
+def expert_pass(place, stack, back, inner):
     block, depth = place.shape[0] // 2, place.shape[1]
     width = stack.shape[1]
     rows, grads = place[:block], place[block:]
@@ -148,23 +151,41 @@
     inner[2] = (swish * up_pre).astype(jnp.bfloat16)
 
 
-def expert(place, stack):
+def expert_kernel(d, place, goals, stack, back, inner, case):
+    me = lax.axis_index("group")
+    lower = (me ^ d) > me
+    full = jnp.max(place[:16, :128].astype(jnp.float32)) < EMPTY / 2
+    sent = functools.reduce(jnp.logical_or, [goals[i] == (me ^ d) for i in range(goals.shape[0])])
+    case[0] = jnp.where(full, jnp.where(lower, 1, 2), 0) + jnp.where(sent, jnp.where(lower, 2, 1), 0)
+
+    @pl.when(full)
+    def _():
+        expert_pass(place, stack, back, inner)
+
+    @pl.when(jnp.logical_not(full))
+    def _():
+        back[...] = jnp.zeros_like(back)
+        inner[...] = jnp.zeros_like(inner)
+
+
+def expert(d, place, goals, stack):
     block, depth = place.shape[0] // 2, place.shape[1]
     width = stack.shape[1]
     return pl.pallas_call(
-        expert_kernel,
+        functools.partial(expert_kernel, d),
         out_shape=[
             jax.ShapeDtypeStruct((block, depth), jnp.bfloat16),
             jax.ShapeDtypeStruct((3, block, width), jnp.bfloat16),
+            SMEM((1,), jnp.int32),
         ],
-        in_specs=[spec(VMEM)] * 2,
-        out_specs=[spec(VMEM)] * 2,
+        in_specs=[spec(VMEM), spec(SMEM), spec(VMEM)],
+        out_specs=[spec(VMEM), spec(VMEM), spec(SMEM)],
         compiler_params=params(),
         cost_estimate=pl.CostEstimate(
             flops=10 * block * depth * width, bytes_accessed=8 * depth * width, transcendentals=block * width
         ),
         name="expert",
-    )(place, stack)
+    )(place, goals, stack)
 
 
 def weights_kernel(count, *refs):
@@ -268,37 +289,51 @@
     return [(i, i ^ d) for i in range(size)]
 
 
-def pass_at(d, order, hops, shape, goals, stack, *packed):
-    nodes, group = lax.axis_size("node"), lax.axis_size("group")
-    stack = lax.ppermute(stack, "node", xor_pairs(nodes, d)) if d else stack
-    places = [
-        lax.ppermute(place, "group", xor_pairs(group, d)) if d else place for d, place in zip(order, packed)
-    ]
-    results = []
-    for place in places:
-        results.append(expert(place, stack))
-        stack, _ = lax.optimization_barrier((stack, results[-1][1]))
-    returned = [
-        lax.ppermute(back, "group", xor_pairs(group, d)) if d else back for d, (back, _) in zip(order, results)
-    ]
-    grads = weights(places, [inner for _, inner in results])
-    grad_tokens = combine(hops, shape, goals, returned)
-    return (grad_tokens, *grads)
+def to_xor(array, d, axis="group"):
+    return lax.ppermute(array, axis, xor_pairs(lax.axis_size(axis), d))
+
+
+def after(array, *others):
+    return lax.optimization_barrier((array, *others))[0]
+
+
+def give_back(case, back, d, beside=lambda: ()):
+    pairs = xor_pairs(lax.axis_size("group"), d)
+    up = [(a, b) for a, b in pairs if a < b]
+    down = [(a, b) for a, b in pairs if a > b]
+
+    def branch(perm):
+        return lambda array: (lax.ppermute(array, "group", perm) if perm else array, beside())
+
+    return lax.switch(case[0], [branch(perm) for perm in ([], up, down, pairs)], back)
 
 
 def on_device(tokens, grad_out, router_gate, counts, routes, partner, w_gate, w_up, w_down):
     nodes, group = lax.axis_size("node"), lax.axis_size("group")
     shape = routes.shape[1:]
     order = sorted(range(1, group), key=lambda d: (d != 2, -d)) + [0]
+    optional = (2, 3) if group == 4 else ()
     hops = [functools.partial(lambda d, me: me ^ d, d) for d in order]
     packed, stack, plan, goals = pack(hops, partner, counts, routes, tokens, grad_out, router_gate, w_gate, w_up, w_down)
-    if nodes > 8:
-        moves = [
-            functools.partial(lax.ppermute, axis_name="node", perm=xor_pairs(nodes, d)) for d in range(1, nodes)
-        ]
-        return pass_at(0, order, hops, shape, goals, lax.switch(plan[0], moves, stack), *packed)
-    branches = [functools.partial(pass_at, d, order, hops, shape) for d in range(1, nodes)]
-    return lax.switch(plan[0], branches, goals, stack, *packed)
+    places = {d: to_xor(place, d) if d else place for d, place in zip(order, packed)}
+    moves = [functools.partial(to_xor, d=d, axis="node") for d in range(1, nodes)]
+    stack = lax.switch(plan[0], moves, stack)
+    inners, returned = {}, {}
+    turns = sorted(order, key=lambda d: (d in optional, d))
+    for d in turns:
+        back, inners[d], case = expert(d, places[d], goals, stack)
+        stack = after(stack, inners[d])
+        if d == 0 or d not in optional:
+            returned[d] = to_xor(back, d) if d else back
+        elif d == optional[0]:
+            returned[d], _ = give_back(case, back, d)
+            stack = after(stack, returned[d])
+        else:
+            beside = lambda: weights([places[d] for d in order], [inners[d] for d in order])
+            returned[d], grads = give_back(case, back, d, beside)
+    if len(optional) < 2:
+        grads = weights([places[d] for d in order], [inners[d] for d in order])
+    return (combine(hops, shape, goals, [returned[d] for d in order]), *grads)
 
 
 def solution(mesh):

time: 79.1 us -> 74.3 us (0.939)
  the two profiles are of different devices: /device:TPU:0 before, /device:TPU:15 now
where the time goes in v4:
time: 74.3 us; the launch traced here: 73.9 us
  waiting for transfers between devices  47.6 us (64%)
  Pallas kernels  15.8 us (21%)
  starting transfers between devices  9.02 us (12%)
  between operations  1.39 us (2%)
    ppermute x5, waiting for transfers between devices, to_xor(): return lax.ppermute(array, axis, xor_pairs(lax.axis_size(axis), d))  34.2 us
    ppermute x2, waiting for transfers between devices, branch(): lax.ppermute(array, 'group', perm)  13.3 us
    pallas_call x4, Pallas kernels, expert(): pl.pallas_call(functools.partial(expert_kernel, d), out_shape=[jax.ShapeD...  8.69 us
    ppermute x2, starting transfers between devices, branch(): lax.ppermute(array, 'group', perm)  4.61 us
    ppermute x5, starting transfers between devices, to_xor(): return lax.ppermute(array, axis, xor_pairs(lax.axis_size(axis), d))  4.41 us
    pallas_call x1, Pallas kernels, weights(): pl.pallas_call(functools.partial(weights_kernel, count), out_shape=[wide,...  4.18 us
    pallas_call x1, Pallas kernels, pack(): pl.pallas_call(functools.partial(pack_kernel, hops, (slots, topk)), out_s...  2.12 us
  transfers between devices with their start and end apart: 7, of which 3 were waited for; matrix products, arithmetic and copies ran while one was open for 0% of the time, Pallas kernels for 17%

profile of v4, /device:TPU:15, one launch (start us, length us, event | category | flops | bytes accessed | tf_op | source)
XLA Modules:
  0.0 73.9 jit_solution(7507798737562207747)
XLA Ops:
  1.3 2.1 %pack.1 = (bf16[256,1024]{1,0:T(8,128)(2,1)S(1)}, bf16[256,1024]{1,0:T(8,128)(2,1)S(1)}, bf16[256,1024]{1,0:T(8,128)(2,1)S(1)}, bf16[256,1024]{1,0:T(8,128)(2,1)...) custom-call(s32[1]{0:T(128)S(6)} %copy.40.counts, s32[8]{0:T(128)} %partner.1, s32[2]{0:T(128)} %bitcast.6, ...), custom_call_target="tpu_custom_call" | custom-call | tf_op jit(solution)/shard_map/pack/pallas_call | solution.py:111
  3.4 0.2 collective-permute-start.14
  3.6 2.3 %collective-permute-start.13 = (bf16[256,1024]{1,0:T(8,128)(2,1)S(1)}, bf16[256,1024]{1,0:T(8,128)(2,1)}, u32[]{:S(2)}, u32[]{:S(2)}) collective-permute-start(bf16[256,1024]{1,0:T(8,128)(2,1)S(1)} %get-tuple-element.174), channel_id=1, source_target_pairs={{0,2},{1,3},{2,0},{3,1},{4,6},{5,7},{6,4},{7,5},{8,10},{9,11},{10,... | collective-permute-start | bytes 1572872 | tf_op jit(solution)/shard_map/ppermute | solution.py:293
  5.9 0.3 collective-permute-start.15
  6.1 35.8 %conditional.3 = (bf16[3072,256]{1,0:T(8,128)(2,1)}) conditional(s32[]{:T(128)} %bitcast.2, bf16[3072,256]{1,0:T(8,128)(2,1)S(1)} %get-tuple-element.176, bf16[3072,256]{1,0:T(8,128)(2,1)S(1)} %get-tuple-element.176, bf16[3072,256]{1,0:T(8,128)(2,1)S(1)} %get-tuple-element.176, ...), branch_computations={%region_0.0_spmd, %region_1.0_spmd, %region_2.0_spmd, %region_3.0_... | conditional | bytes 6291504 | solution.py:320
  6.1 1.6 %collective-permute-start.4 = (bf16[3072,256]{1,0:T(8,128)(2,1)S(1)}, bf16[3072,256]{1,0:T(8,128)(2,1)}, u32[]{:S(2)}, u32[]{:S(2)}) collective-permute-start(bf16[3072,256]{1,0:T(8,128)(2,1)S(1)} %param.4), channel_id=1, source_target_pairs={{0,20},{4,16},{8,28},{12,24},{16,4},{20,0},{24,12},{28,8},{1,21},{... | collective-permute-start | bytes 4718600 | tf_op jit(solution)/shard_map/cond/branch_4_fun/ppermute | solution.py:293
  7.8 34.2 %collective-permute-done.4 = bf16[3072,256]{1,0:T(8,128)(2,1)} collective-permute-done((bf16[3072,256]{1,0:T(8,128)(2,1)S(1)}, bf16[3072,256]{1,0:T(8,128)(2,1)}, u32[]{:S(2)}, u32[]{:S(2)}) %collective-permute-start.4) | collective-permute-done | bytes 1572896 | tf_op jit(solution)/shard_map/cond/branch_4_fun/ppermute | solution.py:293
  42.0 2.6 %expert.4 = (bf16[128,1024]{1,0:T(8,128)(2,1)S(1)}, bf16[3,128,256]{2,1,0:T(8,128)(2,1)S(1)}, s32[1]{0:T(128)S(4)}) custom-call(bf16[256,1024]{1,0:T(8,128)(2,1)S(1)} %get-tuple-element.177.place, s32[2]{0:T(128)S(4)} %get-tuple-element.173.goals, bf16[3072,256]{1,0:T(8,128)(2,1)} %get-tuple-element.214.stack), custom_call_target="tpu_custom_call" | custom-call | flops 335544320 | bytes 2097152 | tf_op jit(solution)/shard_map/expert/pallas_call | solution.py:174
  44.6 0.0 collective-permute-done.14.place
  44.6 1.6 %expert.5 = (bf16[128,1024]{1,0:T(8,128)(2,1)S(1)}, bf16[3,128,256]{2,1,0:T(8,128)(2,1)S(1)}, s32[1]{0:T(128)S(4)}) custom-call(bf16[256,1024]{1,0:T(8,128)(2,1)S(1)} %collective-permute-done.14.place, s32[2]{0:T(128)S(4)} %get-tuple-element.173.goals, bf16[3072,256]{1,0:T(8,128)(2,1)} %get-tuple-element.214.stack), custom_call_target="tpu_custom_call" | custom-call | flops 335544320 | bytes 2097152 | tf_op jit(solution)/shard_map/expert/pallas_call | solution.py:174
  46.2 0.1 collective-permute-start.16
  46.3 0.0 collective-permute-done.13.place
  46.3 2.8 %expert.6 = (bf16[128,1024]{1,0:T(8,128)(2,1)S(1)}, bf16[3,128,256]{2,1,0:T(8,128)(2,1)S(1)}, s32[1]{0:T(128)S(4)}) custom-call(bf16[256,1024]{1,0:T(8,128)(2,1)} %collective-permute-done.13.place, s32[2]{0:T(128)S(4)} %get-tuple-element.173.goals, bf16[3072,256]{1,0:T(8,128)(2,1)} %get-tuple-element.214.stack), custom_call_target="tpu_custom_call" | custom-call | flops 335544320 | bytes 2097152 | tf_op jit(solution)/shard_map/expert/pallas_call | solution.py:174
  49.1 12.3 %conditional.4 = (bf16[128,1024]{1,0:T(8,128)(2,1)S(1)}) conditional(s32[]{:T(128)} %bitcast.3, bf16[128,1024]{1,0:T(8,128)(2,1)S(1)} %get-tuple-element.184, bf16[128,1024]{1,0:T(8,128)(2,1)S(1)} %get-tuple-element.184, bf16[128,1024]{1,0:T(8,128)(2,1)S(1)} %get-tuple-element.184, ...), branch_computations={%region_7.0_spmd, %region_8.0_spmd, %region_9.0_spmd, %region_10.0... | conditional | bytes 1572912 | solution.py:308
  49.1 3.3 %collective-permute-start.7 = (bf16[128,1024]{1,0:T(8,128)(2,1)S(1)}, bf16[128,1024]{1,0:T(8,128)(2,1)S(1)}, u32[]{:S(2)}, u32[]{:S(2)}) collective-permute-start(bf16[128,1024]{1,0:T(8,128)(2,1)S(1)} %param.8), channel_id=1, source_target_pairs={{0,2},{1,3},{4,6},{5,7},{8,10},{9,11},{12,14},{13,15},{16,18},{17,... | collective-permute-start | bytes 786440 | tf_op jit(solution)/shard_map/cond/branch_1_fun/ppermute | solution.py:306
  52.4 8.9 %collective-permute-done.7 = bf16[128,1024]{1,0:T(8,128)(2,1)S(1)} collective-permute-done((bf16[128,1024]{1,0:T(8,128)(2,1)S(1)}, bf16[128,1024]{1,0:T(8,128)(2,1)S(1)}, u32[]{:S(2)}, u32[]{:S(2)}) %collective-permute-start.7) | collective-permute-done | bytes 262176 | tf_op jit(solution)/shard_map/cond/branch_1_fun/ppermute | solution.py:306
  61.3 0.0 collective-permute-done.15.place
  61.3 1.7 %expert.7 = (bf16[128,1024]{1,0:T(8,128)(2,1)S(1)}, bf16[3,128,256]{2,1,0:T(8,128)(2,1)S(1)}, s32[1]{0:T(128)S(4)}) custom-call(bf16[256,1024]{1,0:T(8,128)(2,1)} %collective-permute-done.15.place, s32[2]{0:T(128)S(4)} %get-tuple-element.173.goals, bf16[3072,256]{1,0:T(8,128)(2,1)} %get-tuple-element.214.stack), custom_call_target="tpu_custom_call" | custom-call | flops 335544320 | bytes 2097152 | tf_op jit(solution)/shard_map/expert/pallas_call | solution.py:174
  63.1 10.0 %conditional.5 = (bf16[128,1024]{1,0:T(8,128)(2,1)S(1)}, bf16[1,1024,256]{2,1,0:T(8,128)(2,1)}, bf16[1,1024,256]{2,1,0:T(8,128)(2,1)}, bf16[1,256,1024]{2,1,0:T(8,128)(2,1)}) conditional(s32[]{:T(128)} %bitcast.4, (bf16[256,1024]{1,0:T(8,128)(2,1)}, bf16[256,1024]{1,0:T(8,128)(2,1)}, bf16[256,1024]{1,0:T(8,128)(2,1)S(1)}, ...), branch_computations={%region_11.0_spmd, %region_12.0_spmd, %region_13.0_spmd, %region_1... | conditional | flops 805306368 | bytes 4194376 | solution.py:308
  63.1 1.3 %collective-permute-start.11 = (bf16[128,1024]{1,0:T(8,128)(2,1)S(1)}, bf16[128,1024]{1,0:T(8,128)(2,1)S(1)}, u32[]{:S(2)}, u32[]{:S(2)}) collective-permute-start(bf16[128,1024]{1,0:T(8,128)(2,1)S(1)} %get-tuple-element.120), channel_id=1, source_target_pairs={{2,1},{3,0},{6,5},{7,4},{10,9},{11,8},{14,13},{15,12},{18,17},{19,... | collective-permute-start | bytes 786440 | tf_op jit(solution)/shard_map/cond/branch_2_fun/ppermute | solution.py:306
  64.4 4.2 %weight_grads.6 = (bf16[1,1024,256]{2,1,0:T(8,128)(2,1)}, bf16[1,1024,256]{2,1,0:T(8,128)(2,1)}, bf16[1,256,1024]{2,1,0:T(8,128)(2,1)}) custom-call(bf16[256,1024]{1,0:T(8,128)(2,1)} %get-tuple-element.121.refs_0_, bf16[256,1024]{1,0:T(8,128)(2,1)} %get-tuple-element.122.refs_1_, bf16[256,1024]{1,0:T(8,128)(2,1)S(1)} %get-tuple-element.123.refs_2_, ...), custom_call_target="tpu_custom_call" | custom-call | flops 805306368 | bytes 2621440 | tf_op jit(solution)/shard_map/cond/branch_2_fun/weight_grads/pallas_call | solution.py:210
  68.6 4.4 %collective-permute-done.11 = bf16[128,1024]{1,0:T(8,128)(2,1)S(1)} collective-permute-done((bf16[128,1024]{1,0:T(8,128)(2,1)S(1)}, bf16[128,1024]{1,0:T(8,128)(2,1)S(1)}, u32[]{:S(2)}, u32[]{:S(2)}) %collective-permute-start.11) | collective-permute-done | bytes 262176 | tf_op jit(solution)/shard_map/cond/branch_2_fun/ppermute | solution.py:306
  73.1 0.0 collective-permute-done.16.refs_2_
  73.1 0.8 %combine.1 = bf16[256,1024]{1,0:T(8,128)(2,1)} custom-call(s32[2]{0:T(128)S(4)} %get-tuple-element.173.goals, bf16[128,1024]{1,0:T(8,128)(2,1)S(1)} %get-tuple-element.215.refs_0_, bf16[128,1024]{1,0:T(8,128)(2,1)S(1)} %get-tuple-element.192.refs_1_, bf16[128,1024]{1,0:T(8,128)(2,1)S(1)} %collective-permute-done.16.refs_2_, ...), custom_call_target="tpu_custom_call" | custom-call | tf_op jit(solution)/shard_map/combine/pallas_call | solution.py:277
  (2 shorter events, 0.0 us)
Async XLA Ops:
  3.4 41.2 %collective-permute-start.14 = (bf16[256,1024]{1,0:T(8,128)(2,1)S(1)}, bf16[256,1024]{1,0:T(8,128)(2,1)S(1)}, u32[]{:S(2)}, u32[]{:S(2)}) collective-permute-start(bf16[256,1024]{1,0:T(8,128)(2,1)S(1)} %get-tuple-element.180), channel_id=1, source_target_pairs={{0,1},{1,0},{2,3},{3,2},{4,5},{5,4},{6,7},{7,6},{8,9},{9,8},{10,11... | collective-permute-start | bytes 1572872 | tf_op jit(solution)/shard_map/ppermute | solution.py:293
  3.6 42.7 %collective-permute-start.13 = (bf16[256,1024]{1,0:T(8,128)(2,1)S(1)}, bf16[256,1024]{1,0:T(8,128)(2,1)}, u32[]{:S(2)}, u32[]{:S(2)}) collective-permute-start(bf16[256,1024]{1,0:T(8,128)(2,1)S(1)} %get-tuple-element.174), channel_id=1, source_target_pairs={{0,2},{1,3},{2,0},{3,1},{4,6},{5,7},{6,4},{7,5},{8,10},{9,11},{10,... | collective-permute-start | bytes 1572872 | tf_op jit(solution)/shard_map/ppermute | solution.py:293
  5.9 55.5 %collective-permute-start.15 = (bf16[256,1024]{1,0:T(8,128)(2,1)S(1)}, bf16[256,1024]{1,0:T(8,128)(2,1)}, u32[]{:S(2)}, u32[]{:S(2)}) collective-permute-start(bf16[256,1024]{1,0:T(8,128)(2,1)S(1)} %get-tuple-element.185), channel_id=1, source_target_pairs={{0,3},{1,2},{2,1},{3,0},{4,7},{5,6},{6,5},{7,4},{8,11},{9,10},{10,... | collective-permute-start | bytes 1572872 | tf_op jit(solution)/shard_map/ppermute | solution.py:293
  6.1 35.8 %collective-permute-start.4 = (bf16[3072,256]{1,0:T(8,128)(2,1)S(1)}, bf16[3072,256]{1,0:T(8,128)(2,1)}, u32[]{:S(2)}, u32[]{:S(2)}) collective-permute-start(bf16[3072,256]{1,0:T(8,128)(2,1)S(1)} %param.4), channel_id=1, source_target_pairs={{0,20},{4,16},{8,28},{12,24},{16,4},{20,0},{24,12},{28,8},{1,21},{... | collective-permute-start | bytes 4718600 | tf_op jit(solution)/shard_map/cond/branch_4_fun/ppermute | solution.py:293
  46.2 26.9 %collective-permute-start.16 = (bf16[128,1024]{1,0:T(8,128)(2,1)S(1)}, bf16[128,1024]{1,0:T(8,128)(2,1)S(1)}, u32[]{:S(2)}, u32[]{:S(2)}) collective-permute-start(bf16[128,1024]{1,0:T(8,128)(2,1)S(1)} %get-tuple-element.193), channel_id=1, source_target_pairs={{0,1},{1,0},{2,3},{3,2},{4,5},{5,4},{6,7},{7,6},{8,9},{9,8},{10,11... | collective-permute-start | bytes 786440 | tf_op jit(solution)/shard_map/ppermute | solution.py:293
  49.1 12.2 %collective-permute-start.7 = (bf16[128,1024]{1,0:T(8,128)(2,1)S(1)}, bf16[128,1024]{1,0:T(8,128)(2,1)S(1)}, u32[]{:S(2)}, u32[]{:S(2)}) collective-permute-start(bf16[128,1024]{1,0:T(8,128)(2,1)S(1)} %param.8), channel_id=1, source_target_pairs={{0,2},{1,3},{4,6},{5,7},{8,10},{9,11},{12,14},{13,15},{16,18},{17,... | collective-permute-start | bytes 786440 | tf_op jit(solution)/shard_map/cond/branch_1_fun/ppermute | solution.py:306
  63.1 9.9 %collective-permute-start.11 = (bf16[128,1024]{1,0:T(8,128)(2,1)S(1)}, bf16[128,1024]{1,0:T(8,128)(2,1)S(1)}, u32[]{:S(2)}, u32[]{:S(2)}) collective-permute-start(bf16[128,1024]{1,0:T(8,128)(2,1)S(1)} %get-tuple-element.120), channel_id=1, source_target_pairs={{2,1},{3,0},{6,5},{7,4},{10,9},{11,8},{14,13},{15,12},{18,17},{19,... | collective-permute-start | bytes 786440 | tf_op jit(solution)/shard_map/cond/branch_2_fun/ppermute | solution.py:306
